TPU v7x, 256 devices: a whole 4x4x8 slice. The times are simulated.
256 devices in a mesh: dep: 128 (over z, x, y), tp: 2 (over core).
Axes of the slice: x: 4, y: 4, z: 8, core: 2. Of those that a mesh axis runs over, the one named last changes fastest.
Arguments:
- patches: bfloat16 [65536, 1152], P('dep', 'tp'), may hold values from -36 to 36
- image_count: int32 [128], P('dep'), may hold values from 0 to 1, as said below
- text_tokens: bfloat16 [16384, 4096], P('dep', 'tp'), may hold values from -6 to 6
- norm_gain: float32 [1152], replicated, may hold values from 0.1 to 1.9
- norm_bias: float32 [1152], replicated, may hold values from -3 to 3
- patch_proj: bfloat16 [1152, 3, 576], P(None, None, 'tp')
- patch_out: bfloat16 [576, 1152], P('tp'), may hold values from -0.25 to 0.25
- merge_gain: float32 [1152], replicated, may hold values from 0.1 to 1.9
- merge_bias: float32 [1152], replicated, may hold values from -3 to 3
- merger: bfloat16 [4, 1152, 4096], P(None, 'tp', 'dep'), may hold values from -1 to 1
- token_gain: float32 [4096], P('tp'), may hold values from 0.1 to 1.9
- router: bfloat16 [4096, 128], P('tp')
- expert_ids: int32 [16384, 8], P('dep'), may hold values from 0 to 127, as said below
Outputs:
- dispatched: bfloat16 [128, 2048, 4096], P('dep', None, 'tp')
- gate_probs: float32 [16384, 8], P('dep')
Inputs may be any that keep to these rules, and one draw needn't show every extreme that they name: `image_count`: in each aligned pair of dep indices (2k, 2k+1) exactly one holds an image. `expert_ids`: among the rows of one index of dep exactly 64 experts are named, each exactly 16 times. One expert is named by the rows of every index of dep, another by the rows of a single index only.
All inputs are finite; a program needn't handle non-finite values.
Results may differ from a plain program's by a relative error of at most 0.013.
Values may be sent and summed in bfloat16 or wider, within the bound.
A program may use at most 192 MiB of HBM per device.

v0:
```python
import math

import jax
import jax.numpy as jnp
from jax import lax
from jax.sharding import PartitionSpec as P

VISION_HEAD_SIZE = 72
D = 4096


EPS = 1e-06


def layer_stats_norm(values_in, gain_vec, bias_vec):
    feature_count = values_in.shape[-1]
    row_mean = jnp.sum(values_in, -1, keepdims=True) / feature_count
    row_var = (
        jnp.sum(values_in * values_in, -1, keepdims=True) / feature_count - row_mean * row_mean
    )
    return (values_in - row_mean) * lax.rsqrt(row_var + EPS) * gain_vec + bias_vec


def attend(query_rows, key_matrix, value_matrix, head_count):
    row_count = query_rows.shape[0]
    head_depth = query_rows.shape[1] // head_count
    query_per_head = query_rows.reshape(row_count, head_count, head_depth)
    key_per_head = key_matrix.reshape(key_matrix.shape[0], head_count, head_depth)
    value_per_head = value_matrix.reshape(value_matrix.shape[0], head_count, head_depth)
    attention_logits = jnp.einsum(
        "ylj,glj->lyg", query_per_head, key_per_head, preferred_element_type=jnp.float32
    ) / math.sqrt(head_depth)
    attention_weights = jax.nn.softmax(attention_logits, axis=-1).astype(jnp.bfloat16)
    attended_output = jnp.einsum(
        "irs,siy->riy", attention_weights, value_per_head, preferred_element_type=jnp.float32
    )
    return attended_output.reshape(row_count, head_count * head_depth).astype(jnp.bfloat16)


def per_device(
    patches,
    image_count,
    text_tokens,
    norm_gain,
    norm_bias,
    patch_proj,
    patch_out,
    merge_gain,
    merge_bias,
    merger,
    token_gain,
    router,
    expert_ids,
):
    tp_index = lax.axis_index("tp")
    half_width = patches.shape[1]
    has_image = image_count[0] == 1
    gathered = lax.all_gather(patches, "tp", axis=1, tiled=True)
    pixels_in = gathered.astype(jnp.float32)
    normed_in = layer_stats_norm(pixels_in, norm_gain, norm_bias).astype(jnp.bfloat16)
    band_width = patch_proj.shape[2]
    projected = jnp.dot(
        normed_in,
        patch_proj.reshape(patch_proj.shape[0], 3 * band_width),
        preferred_element_type=jnp.float32,
    ).astype(jnp.bfloat16)
    query_rows = projected[:, :band_width]
    key_matrix = projected[:, band_width : 2 * band_width]
    value_matrix = projected[:, 2 * band_width :]
    attended_output = attend(query_rows, key_matrix, value_matrix, band_width // VISION_HEAD_SIZE)
    attended = lax.psum_scatter(
        jnp.dot(attended_output, patch_out, preferred_element_type=jnp.float32),
        "tp",
        scatter_dimension=1,
        tiled=True,
    )
    residual = lax.dynamic_slice_in_dim(pixels_in, tp_index * half_width, half_width, 1) + attended
    row_sums = lax.psum((jnp.sum(residual, -1), jnp.sum(residual * residual, -1)), "tp")
    full_width = 2 * half_width
    row_mean = row_sums[0] / full_width
    row_var = row_sums[1] / full_width - row_mean * row_mean
    gain_half = lax.dynamic_slice_in_dim(merge_gain, tp_index * half_width, half_width, 0)
    bias_half = lax.dynamic_slice_in_dim(merge_bias, tp_index * half_width, half_width, 0)
    merged_in = (
        (residual - row_mean[:, None]) * lax.rsqrt(row_var + EPS)[:, None] * gain_half + bias_half
    ).astype(jnp.bfloat16)
    premerge = merged_in.reshape(merged_in.shape[0] // 4, 4 * half_width)
    shard_piece = lax.all_gather(merger, "dep", axis=2, tiled=True)
    partial_terms = jnp.dot(
        premerge,
        shard_piece.reshape(4 * half_width, shard_piece.shape[2]),
        preferred_element_type=jnp.float32,
    )
    merged_rows = lax.psum_scatter(partial_terms, "tp", scatter_dimension=1, tiled=True).astype(
        jnp.bfloat16
    )
    visual_count = merged_rows.shape[0]
    visual_head = jnp.where(has_image, merged_rows, text_tokens)
    hidden = jnp.concatenate([visual_head, text_tokens[visual_count:]], 0)
    hidden_f = hidden.astype(jnp.float32)
    scaled = hidden_f * token_gain
    partial_logits = jnp.dot(
        scaled.astype(jnp.bfloat16), router, preferred_element_type=jnp.float32
    )
    logit_sum, square_sum = lax.psum((partial_logits, jnp.sum(hidden_f * hidden_f, -1)), "tp")
    inv_rms = lax.rsqrt(square_sum / D + EPS)[:, None]
    logits = logit_sum * inv_rms
    normed = (scaled * inv_rms).astype(jnp.bfloat16)
    chosen = jnp.take_along_axis(logits, expert_ids, 1)
    gate_probs = jax.nn.softmax(chosen, axis=-1)
    token_count = expert_ids.shape[0]
    top_count = expert_ids.shape[1]
    expert_count = router.shape[1]
    slot_count = 2 * token_count * top_count // expert_count
    flat_ids = expert_ids.reshape(-1)
    onehot = (flat_ids[:, None] == jnp.arange(expert_count, dtype=jnp.int32)[None, :]).astype(
        jnp.int32
    )
    before = jnp.cumsum(onehot, 0) - onehot
    slot_rank = jnp.sum(before * onehot, 1)
    target = flat_ids * slot_count + slot_rank
    sources = jnp.arange(token_count * top_count, dtype=jnp.int32) // top_count
    buffer = (
        jnp.zeros((expert_count * slot_count, normed.shape[1]), jnp.bfloat16)
        .at[target]
        .set(normed[sources])
    )
    outgoing = buffer.reshape(expert_count, slot_count, normed.shape[1])
    dispatched = lax.all_to_all(outgoing, "dep", split_axis=0, concat_axis=1, tiled=True)
    return (dispatched, gate_probs)


def solution(mesh):
    return jax.shard_map(
        per_device,
        mesh=mesh,
        in_specs=(
            P("dep", "tp"),
            P("dep"),
            P("dep", "tp"),
            P(),
            P(),
            P(None, None, "tp"),
            P("tp", None),
            P(),
            P(),
            P(None, "tp", "dep"),
            P("tp"),
            P("tp", None),
            P("dep", None),
        ),
        out_specs=(P("dep", None, "tp"), P("dep", None)),
        check_vma=False,
    )
```

profile of v0, /device:TPU:1, one launch (start us, length us, event | category | flops | bytes accessed | tf_op | source)
XLA Modules:
  0.0 511.4 jit_solution(3499946391822689987)
XLA Ops:
  8.1 0.7 all-gather.3.cloned.1.call-update
  8.8 21.0 %all-gather.3.cloned.1.call-done = bf16[512,1152]{0,1:T(8,128)(2,1)} async-done(((bf16[512,576]{0,1:T(8,128)(2,1)}), bf16[512,1152]{0,1:T(8,128)(2,1)}) %all-gather.3.cloned.1.call-update) | async-done | bytes 1179664 | tf_op jit(solution)/shard_map/all_gather | solution.py:58
  29.8 1.6 convert_reduce_fusion
  31.4 2.7 convolution_convert_fusion
  34.2 0.1 fusion.33
  34.2 3.5 fusion.34
  37.7 2.7 fusion.11
  40.5 2.2 fusion.35
  42.8 0.0 all-gather.5.cloned.1.call-start
  42.9 0.7 copy.52
  43.6 0.0 reduce-scatter.5.cloned.1.call-start
  43.7 0.1 dynamic_slice.10
  43.8 0.1 dynamic_slice.11
  43.9 1.8 convert_element_type.45
  45.6 13.7 %reduce-scatter.3.cloned.1.call-done = f32[512,576]{0,1:T(8,128)} async-done(((f32[512,1152]{0,1:T(8,128)}), f32[512,576]{0,1:T(8,128)}) %reduce-scatter.3.cloned.1.call-update) | async-done | bytes 1179664 | tf_op jit(solution)/shard_map/reduce_scatter | solution.py:71
  59.3 2.0 fusion.32
  61.3 2.5 all-reduce
  63.8 0.2 add_convert_fusion.2
  64.0 0.3 copy.51
  64.3 0.6 reshape.165
  65.0 146.9 %all-gather.5.cloned.1.call-done = bf16[4,576,4096]{1,0,2:T(4,128)(2,1)} async-done(((bf16[4,576,32]{1,0,2:T(4,128)(2,1)}), bf16[4,576,4096]{1,0,2:T(4,128)(2,1)}) %all-gather.5.cloned.1.call-update) | async-done | bytes 18874384 | tf_op jit(solution)/shard_map/all_gather | solution.py:88
  211.9 32.1 %copy.53 = bf16[4,576,4096]{2,1,0:T(8,128)(2,1)} copy(bf16[4,576,4096]{1,0,2:T(4,128)(2,1)} %all-gather.5.cloned.1.call-done) | data formatting | bytes 37748736 | tf_op jit(solution)/shard_map/all_gather | solution.py:88
  244.0 10.3 %fusion.36 = f32[128,4096]{1,0:T(8,128)} fusion(bf16[128,2304]{1,0:T(8,128)(2,1)S(1)} %reshape.165, bf16[2304,4096]{1,0:T(8,128)(2,1)} %bitcast.40), kind=kOutput, calls=%fused_computation.71 | convolution fusion | flops 2415919104 | bytes 21561344 | tf_op jit(solution)/shard_map/dot_general | solution.py:89
  254.3 0.1 copy.46
  254.4 0.1 eq.35
  254.5 0.1 eq.31
  255.3 0.1 copy.48
  255.4 0.2 fusion.23
  255.7 0.1 copy.49
  255.8 0.1 copy.45
  255.9 0.1 mul.102
  256.0 0.4 fusion.21
  256.4 11.2 %reduce-scatter.5.cloned.1.call-done = f32[128,2048]{1,0:T(8,128)} async-done(((f32[128,4096]{1,0:T(8,128)}), f32[128,2048]{1,0:T(8,128)}) %reduce-scatter.5.cloned.1.call-update) | async-done | bytes 1048592 | tf_op jit(solution)/shard_map/reduce_scatter | solution.py:94
  267.6 1.5 fusion.17
  269.1 2.5 psum.30
  271.5 0.2 fusion.16
  271.7 25.1 %scatter_custom_fusion = bf16[2048,2048]{1,0:T(8,128)(2,1)} fusion(s32[1024]{0:T(1024)S(1)} %bitcast.48, bf16[128,2048]{1,0:T(8,128)(2,1)S(1)} %fusion.16, s32[1024]{0:T(1024)S(1)} %broadcast_clamp_fusion, bf16[]{:T(256)} %constant.27.clone.1), kind=kCustom, calls=%fused_computation.4 | custom fusion | bytes 8388610 | tf_op jit(solution)/shard_map/scatter | solution.py:126
  296.8 14.4 %all-to-all-start = ((bf16[128,16,2048]{2,1,0:T(8,128)(2,1)}), bf16[128,16,2048]{2,1,0:T(8,128)(2,1)}, u32[]{:S(2)}, u32[]{:S(2)}) async-start(bf16[128,16,2048]{2,1,0:T(8,128)(2,1)} %bitcast.41), calls=%async_computation.2 | async-start | bytes 16777216 | tf_op jit(solution)/shard_map/all_to_all | solution.py:129
  311.2 0.9 fusion.18
  312.2 0.1 copy.54
  312.3 0.1 reshape.177
  312.4 31.8 %all-reduce.3.cloned.1.call-done = f32[128,128]{1,0:T(8,128)} async-done(((f32[128,128]{1,0:T(8,128)}), f32[128,128]{1,0:T(8,128)}) %all-reduce.3.cloned.1.call-update) | async-done | bytes 65552 | tf_op jit(solution)/shard_map/psum | solution.py:105
  344.2 0.9 broadcast_multiply_fusion
  345.1 6.8 %gather_fusion = f32[1024]{0:T(1024)S(1)} fusion(f32[128,128]{1,0:T(8,128)S(1)} %broadcast_multiply_fusion, s32[1024]{0:T(1024)S(1)} %reshape.177), kind=kCustom, calls=%fused_computation.1 | custom fusion | bytes 16384 | tf_op jit(solution)/shard_map/jit(take_along_axis)/gather | solution.py:109
  351.9 0.1 reshape.180
  352.1 0.6 fusion.28
  352.7 142.9 %all-to-all-done = bf16[128,16,2048]{2,1,0:T(8,128)(2,1)} async-done(((bf16[128,16,2048]{2,1,0:T(8,128)(2,1)}), bf16[128,16,2048]{2,1,0:T(8,128)(2,1)}, u32[]{:S(2)}, u32[]{:S(2)}) %all-to-all-start) | async-done | bytes 8388640 | tf_op jit(solution)/shard_map/all_to_all | solution.py:129
  495.7 8.6 %copy.60 = bf16[1,2048,2048]{2,1,0:T(8,128)(2,1)} copy(bf16[1,2048,2048]{2,1,0:T(8,128)(2,1)} %bitcast.15) | data formatting | bytes 16777216
  (44 shorter events, 0.5 us)
Async XLA Ops:
  8.0 23.4 %copy-start = (bf16[1152,3,288]{0,2,1:T(8,128)(2,1)S(1)}, bf16[1152,3,288]{0,2,1:T(8,128)(2,1)}, u32[]{:S(2)}) copy-start(bf16[1152,3,288]{0,2,1:T(8,128)(2,1)} %param.18) | copy-start | bytes 5971972
  8.0 21.8 %all-gather.3.cloned.1.call-start = ((), (), s32[]{:S(2)}) async-start(), calls=%async_computation.3 | async-start | bytes 1769472 | tf_op jit(solution)/shard_map/all_gather | solution.py:58
  8.7 50.5 %reduce-scatter.3.cloned.1.call-start = ((), (), s32[]{:S(2)}) async-start(), calls=%async_computation.4 | async-start | bytes 3538944 | tf_op jit(solution)/shard_map/reduce_scatter | solution.py:71
  37.7 2.8 copy-start.3
  40.5 2.4 copy-start.6
  40.5 3.2 copy-start.9
  40.5 3.3 copy-start.10
  40.5 3.3 copy-start.2
  42.8 169.1 %all-gather.5.cloned.1.call-start = ((), (), s32[]{:S(2)}) async-start(), calls=%async_computation.5 | async-start | bytes 21135360 | tf_op jit(solution)/shard_map/all_gather | solution.py:88
  43.6 223.9 %reduce-scatter.5.cloned.1.call-start = ((), (), s32[]{:S(2)}) async-start(), calls=%async_computation.6 | async-start | bytes 3145728 | tf_op jit(solution)/shard_map/reduce_scatter | solution.py:94
  244.0 10.3 %copy-start.7 = (s32[128,8]{0,1:T(8,128)S(1)}, s32[128,8]{0,1:T(8,128)}, u32[]{:S(2)}) copy-start(s32[128,8]{0,1:T(8,128)} %param.25) | copy-start | bytes 12292
  254.3 13.3 %copy-start.5 = (bf16[128,2048]{1,0:T(8,128)(2,1)S(1)}, bf16[128,2048]{1,0:T(8,128)(2,1)}, u32[]{:S(2)}) copy-start(bf16[128,2048]{1,0:T(8,128)(2,1)} %param.15) | copy-start | bytes 1572868
  255.6 15.9 %copy-start.8 = (f32[2048]{0:T(1024)S(1)}, f32[2048]{0:T(1024)}, u32[]{:S(2)}) copy-start(f32[2048]{0:T(1024)} %param.23) | copy-start | bytes 24580
  296.8 14.4 %copy-start.4 = (bf16[2048,128]{1,0:T(8,128)(2,1)S(1)}, bf16[2048,128]{1,0:T(8,128)(2,1)}, u32[]{:S(2)}) copy-start(bf16[2048,128]{1,0:T(8,128)(2,1)} %param.24) | copy-start | bytes 1572868
  296.8 198.9 %all-to-all-start = ((bf16[128,16,2048]{2,1,0:T(8,128)(2,1)}), bf16[128,16,2048]{2,1,0:T(8,128)(2,1)}, u32[]{:S(2)}, u32[]{:S(2)}) async-start(bf16[128,16,2048]{2,1,0:T(8,128)(2,1)} %bitcast.41), calls=%async_computation.2 | async-start | bytes 16777216 | tf_op jit(solution)/shard_map/all_to_all | solution.py:129
  311.2 33.0 %all-reduce.3.cloned.1.call-start = ((), (), s32[]{:S(2)}) async-start(), calls=%async_computation.7 | async-start | bytes 131072 | tf_op jit(solution)/shard_map/psum | solution.py:105
  495.7 8.6 %copy-start.1 = (bf16[1152,3,288]{0,2,1:T(8,128)(2,1)S(1)}, bf16[1152,3,288]{0,2,1:T(8,128)(2,1)}, u32[]{:S(2)}) copy-start(bf16[1152,3,288]{0,2,1:T(8,128)(2,1)} %param.18) | copy-start | bytes 5971972
Sparse Core Ops, SparseCore 0:
  10.6 19.0 all-gather.2
  42.9 16.3 reduce-scatter.2
  254.4 13.1 reduce-scatter.4
  314.2 29.8 all-reduce.2
Sparse Core Ops, SparseCore 1:
  47.3 164.5 all-gather.4
where the time goes:
time: 515 us; the launch traced here: 511 us
  waiting for transfers between devices  368 us (71%)
  local copies, waits for them, and re-layouts  75.5 us (15%)
  matrix products  22.4 us (4%)
  between operations  16.1 us (3%)
  starting transfers between devices  14.6 us (3%)
  other arithmetic  9.54 us (2%)
    all_gather x1, waiting for transfers between devices, per_device(): shard_piece = lax.all_gather(merger, 'dep', axis=2, tiled=True)  147 us
    all_to_all x1, waiting for transfers between devices, per_device(): lax.all_to_all(outgoing, 'dep', split_axis=0, concat_axis=1, tiled=True)  143 us
    all_gather x1, local copies, waits for them, and re-layouts, per_device(): shard_piece = lax.all_gather(merger, 'dep', axis=2, tiled=True)  32.1 us
    psum x1, waiting for transfers between devices, per_device(): lax.psum((partial_logits, jnp.sum(hidden_f * hidden_f, -1)), 'tp')  31.8 us
    scatter x1, local copies, waits for them, and re-layouts, per_device(): buffer = jnp.zeros((expert_count * slot_count, normed.shape[1]), jnp.bflo...  25.1 us
    all_gather x1, waiting for transfers between devices, per_device(): gathered = lax.all_gather(patches, 'tp', axis=1, tiled=True)  21 us
    all_to_all x1, starting transfers between devices, per_device(): lax.all_to_all(outgoing, 'dep', split_axis=0, concat_axis=1, tiled=True)  14.4 us
    reduce_scatter x1, waiting for transfers between devices, per_device(): lax.psum_scatter(jnp.dot(attended_output, patch_out, preferred_element_ty...  13.7 us
  transfers between devices with their start and end apart: 6, of which 6 were waited for; matrix products, arithmetic and copies ran while one was open for 3% of the time, Pallas kernels for 0%

commit v1 on v0

--- a/solution.py
+++ b/solution.py
@@ -3,7 +3,17 @@
 import jax
 import jax.numpy as jnp
 from jax import lax
+from jax.experimental import pallas as pl
+from jax.experimental.pallas import tpu as pltpu
 from jax.sharding import PartitionSpec as P
+
+MESH = pl.DeviceIdType.MESH
+NZ = 8
+NX = 4
+NY = 4
+PLANE = NX * NY
+SLOTS = 16
+ROWS = 128
 
 VISION_HEAD_SIZE = 72
 D = 4096
@@ -35,6 +45,153 @@
         "irs,siy->riy", attention_weights, value_per_head, preferred_element_type=jnp.float32
     )
     return attended_output.reshape(row_count, head_count * head_depth).astype(jnp.bfloat16)
+
+
+def selection(ids, first_expert):
+    experts = first_expert + lax.broadcasted_iota(jnp.int32, (PLANE, ROWS), 0)
+    count = jnp.zeros((PLANE, ROWS), jnp.float32)
+    for k in range(ids.shape[0]):
+        count += (ids[k : k + 1, :] == experts).astype(jnp.float32)
+    earlier = (
+        lax.broadcasted_iota(jnp.int32, (ROWS, ROWS), 0)
+        < lax.broadcasted_iota(jnp.int32, (ROWS, ROWS), 1)
+    ).astype(jnp.bfloat16)
+    before = jnp.dot(count.astype(jnp.bfloat16), earlier, preferred_element_type=jnp.float32)
+    slot = lax.broadcasted_iota(jnp.int32, (PLANE, SLOTS, ROWS), 1).astype(jnp.float32)
+    first = before[:, None, :]
+    last = (before + count)[:, None, :]
+    chosen = (slot >= first) & (slot < last)
+    return jnp.where(chosen, 1.0, 0.0).astype(jnp.bfloat16).reshape(PLANE * SLOTS, ROWS)
+
+
+def dispatch_kernel(
+    rows_ref, ids_ref, out_ref, held, held_ids, stage, ring_send, ring_recv, ids_send, ids_recv, out_send, out_recv
+):
+    dep = lax.axis_index("dep")
+    z = dep // PLANE
+    xy = lax.rem(dep, PLANE)
+    x = xy // NY
+    y = lax.rem(xy, NY)
+    width = rows_ref.shape[1]
+    half = width // 2
+
+    def along_z(step):
+        return {"dep": lax.rem(z + step, NZ) * PLANE + xy}
+
+    def in_plane(step):
+        to_x = lax.rem(x + step // NY, NX)
+        to_y = lax.rem(y + lax.rem(step, NY), NY)
+        return to_x * NY + to_y
+
+    barrier = pltpu.get_barrier_semaphore()
+    for step in range(1, NZ):
+        pl.semaphore_signal(barrier, inc=1, device_id=along_z(step), device_id_type=MESH)
+
+    def greet(step, carry):
+        pl.semaphore_signal(
+            barrier, inc=1, device_id={"dep": z * PLANE + in_plane(step)}, device_id_type=MESH
+        )
+        return carry
+
+    lax.fori_loop(1, PLANE, greet, 0)
+    pl.semaphore_wait(barrier, NZ - 1 + PLANE - 1)
+
+    id_copies = []
+    for step in range(1, NZ):
+        copy = pltpu.make_async_remote_copy(
+            src_ref=ids_ref,
+            dst_ref=held_ids.at[NZ - step],
+            send_sem=ids_send.at[step],
+            recv_sem=ids_recv.at[NZ - step],
+            device_id=along_z(step),
+            device_id_type=MESH,
+        )
+        copy.start()
+        id_copies.append(copy)
+
+    def hop(number, source, slot, columns, step):
+        copy = pltpu.make_async_remote_copy(
+            src_ref=source.at[:, columns],
+            dst_ref=held.at[slot, :, columns],
+            send_sem=ring_send.at[number],
+            recv_sem=ring_recv.at[number],
+            device_id=along_z(step),
+            device_id_type=MESH,
+        )
+        copy.start()
+        return copy
+
+    every = pl.ds(0, width)
+
+    def spread(slot, source, ids):
+        chosen = selection(ids, z * PLANE)
+        for c in range(0, width, 512):
+            stage[slot, :, c : c + 512] = jnp.dot(
+                chosen, source[:, c : c + 512], preferred_element_type=jnp.float32
+            ).astype(jnp.bfloat16)
+        at_dest = (lax.rem(z + slot, NZ) * PLANE + xy) * SLOTS
+        own = pltpu.make_async_copy(
+            stage.at[slot, pl.ds(xy * SLOTS, SLOTS)], out_ref.at[pl.ds(at_dest, SLOTS)], out_recv
+        )
+        own.start()
+
+        def send(step, carry):
+            peer = in_plane(step)
+            pltpu.make_async_remote_copy(
+                src_ref=stage.at[slot, pl.ds(peer * SLOTS, SLOTS)],
+                dst_ref=out_ref.at[pl.ds(at_dest, SLOTS)],
+                send_sem=out_send,
+                recv_sem=out_recv,
+                device_id={"dep": z * PLANE + peer},
+                device_id_type=MESH,
+            ).start()
+            return carry
+
+        lax.fori_loop(1, PLANE, send, 0)
+
+    right = hop(0, rows_ref, NZ - 1, every, 1)
+    left = hop(4, rows_ref, 1, every, NZ - 1)
+    spread(0, rows_ref, ids_ref[...])
+    for step in range(1, 5):
+        back, ahead = NZ - step, step
+        right.wait()
+        left.wait()
+        if step < 3:
+            right = hop(step, held.at[back], back - 1, every, 1)
+            left = hop(4 + step, held.at[ahead], ahead + 1, every, NZ - 1)
+        if step == 3:
+            right = hop(3, held.at[back], back - 1, pl.ds(0, half), 1)
+            left = hop(7, held.at[ahead], ahead + 1, pl.ds(half, half), NZ - 1)
+        for slot in (back, ahead) if back != ahead else (back,):
+            id_copies[NZ - 1 - slot].wait()
+            spread(slot, held.at[slot], held_ids[slot])
+    sent = stage.at[:, pl.ds(0, (PLANE - 1) * SLOTS)]
+    pltpu.make_async_copy(sent, sent, out_send).wait()
+    pltpu.make_async_copy(out_ref, out_ref, out_recv).wait()
+
+
+def dispatch(normed, expert_ids):
+    width = normed.shape[1]
+    return pl.pallas_call(
+        dispatch_kernel,
+        out_shape=jax.ShapeDtypeStruct((NZ * PLANE * SLOTS, width), jnp.bfloat16),
+        in_specs=[pl.BlockSpec(memory_space=pltpu.VMEM)] * 2,
+        out_specs=pl.BlockSpec(memory_space=pl.ANY),
+        scratch_shapes=[
+            pltpu.VMEM((NZ, ROWS, width), jnp.bfloat16),
+            pltpu.VMEM((NZ, 8, ROWS), jnp.int32),
+            pltpu.VMEM((NZ, PLANE * SLOTS, width), jnp.bfloat16),
+            pltpu.SemaphoreType.DMA((8,)),
+            pltpu.SemaphoreType.DMA((8,)),
+            pltpu.SemaphoreType.DMA((8,)),
+            pltpu.SemaphoreType.DMA((8,)),
+            pltpu.SemaphoreType.DMA,
+            pltpu.SemaphoreType.DMA,
+        ],
+        compiler_params=pltpu.CompilerParams(
+            collective_id=0, has_side_effects=True, vmem_limit_bytes=48 * 1024 * 1024
+        ),
+    )(normed, expert_ids.T)
 
 
 def per_device(
@@ -108,25 +265,7 @@
     normed = (scaled * inv_rms).astype(jnp.bfloat16)
     chosen = jnp.take_along_axis(logits, expert_ids, 1)
     gate_probs = jax.nn.softmax(chosen, axis=-1)
-    token_count = expert_ids.shape[0]
-    top_count = expert_ids.shape[1]
-    expert_count = router.shape[1]
-    slot_count = 2 * token_count * top_count // expert_count
-    flat_ids = expert_ids.reshape(-1)
-    onehot = (flat_ids[:, None] == jnp.arange(expert_count, dtype=jnp.int32)[None, :]).astype(
-        jnp.int32
-    )
-    before = jnp.cumsum(onehot, 0) - onehot
-    slot_rank = jnp.sum(before * onehot, 1)
-    target = flat_ids * slot_count + slot_rank
-    sources = jnp.arange(token_count * top_count, dtype=jnp.int32) // top_count
-    buffer = (
-        jnp.zeros((expert_count * slot_count, normed.shape[1]), jnp.bfloat16)
-        .at[target]
-        .set(normed[sources])
-    )
-    outgoing = buffer.reshape(expert_count, slot_count, normed.shape[1])
-    dispatched = lax.all_to_all(outgoing, "dep", split_axis=0, concat_axis=1, tiled=True)
+    dispatched = dispatch(normed, expert_ids)[None]
     return (dispatched, gate_probs)
 
 

time: 515 us -> 403 us (0.78)
  waiting for transfers between devices: 368 us -> 195 us
  Pallas kernels: 0 us -> 103 us
  local copies, waits for them, and re-layouts: 75.5 us -> 49.7 us
  starting transfers between devices: 14.6 us -> 0.2 us
    all_to_all x1 -> x0, waiting for transfers between devices: 143 us -> none  [per_device(): lax.all_to_all(outgoing, 'dep', split_axis=0, concat_axis=1, tiled=True)]
    pallas_call x0 -> x1, Pallas kernels: none -> 103 us  [dispatch(): pl.pallas_call(dispatch_kernel, out_shape=jax.ShapeDtypeStruct((NZ * PLAN...]
    psum x1, waiting for transfers between devices: 31.8 us -> 0.02 us  [per_device(): lax.psum((partial_logits, jnp.sum(hidden_f * hidden_f, -1)), 'tp')]
    scatter x1 -> x0, local copies, waits for them, and re-layouts: 25.1 us -> none  [per_device(): buffer = jnp.zeros((expert_count * slot_count, normed.shape[1]), jnp.bflo...]
    all_to_all x1 -> x0, starting transfers between devices: 14.4 us -> none  [per_device(): lax.all_to_all(outgoing, 'dep', split_axis=0, concat_axis=1, tiled=True)]
  transfers between devices with their start and end apart: 6 -> 5, of which waited for: 6 -> 4; matrix products, arithmetic and copies ran while one was open for 3% -> 2% of each run, Pallas kernels for 0% -> 26%
where the time goes in v1:
time: 403 us; the launch traced here: 401 us
  waiting for transfers between devices  195 us (48%)
  Pallas kernels  103 us (26%)
  local copies, waits for them, and re-layouts  49.7 us (12%)
  matrix products  22.6 us (6%)
  between operations  16.1 us (4%)
  other arithmetic  8.9 us (2%)
  blocking collectives  5.13 us (1%)
    all_gather x1, waiting for transfers between devices, per_device(): shard_piece = lax.all_gather(merger, 'dep', axis=2, tiled=True)  147 us
    pallas_call x1, Pallas kernels, dispatch(): pl.pallas_call(dispatch_kernel, out_shape=jax.ShapeDtypeStruct((NZ * PLAN...  103 us
    all_gather x1, local copies, waits for them, and re-layouts, per_device(): shard_piece = lax.all_gather(merger, 'dep', axis=2, tiled=True)  32.1 us
    all_gather x1, waiting for transfers between devices, per_device(): gathered = lax.all_gather(patches, 'tp', axis=1, tiled=True)  21 us
    reduce_scatter x1, waiting for transfers between devices, per_device(): lax.psum_scatter(jnp.dot(attended_output, patch_out, preferred_element_ty...  13.7 us
    reduce_scatter x1, waiting for transfers between devices, per_device(): lax.psum_scatter(partial_terms, 'tp', scatter_dimension=1, tiled=True)  12.3 us
    dot_general x1, matrix products, per_device(): jnp.dot(premerge, shard_piece.reshape(4 * half_width, shard_piece.shape[2...  10.5 us
    unnamed x24, local copies, waits for them, and re-layouts  9.38 us
  transfers between devices with their start and end apart: 5, of which 4 were waited for; matrix products, arithmetic and copies ran while one was open for 2% of the time, Pallas kernels for 26%

profile of v1, /device:TPU:1, one launch (start us, length us, event | category | flops | bytes accessed | tf_op | source)
XLA Modules:
  0.0 400.9 jit_solution(12996661887737032046)
XLA Ops:
  8.0 0.0 copy-start
  8.0 0.0 all-gather.3.cloned.1.call-start
  8.1 0.7 all-gather.3.cloned.1.call-update
  8.7 0.0 reduce-scatter.3.cloned.1.call-start
  8.8 21.0 %all-gather.3.cloned.1.call-done = bf16[512,1152]{0,1:T(8,128)(2,1)} async-done(((bf16[512,576]{0,1:T(8,128)(2,1)}), bf16[512,1152]{0,1:T(8,128)(2,1)}) %all-gather.3.cloned.1.call-update) | async-done | bytes 1179664 | tf_op jit(solution)/shard_map/all_gather | solution.py:215
  29.8 1.6 convert_reduce_fusion
  31.4 2.7 convolution_convert_fusion
  34.2 0.1 fusion.25
  34.2 3.5 fusion.26
  37.7 2.7 fusion.8
  40.5 0.0 copy-start.7
  40.5 0.0 copy-start.9
  40.5 0.0 copy-start.10
  40.5 2.2 fusion.27
  42.8 0.0 reduce-scatter.3.cloned.1.call-update
  42.8 0.0 all-gather.5.cloned.1.call-start
  42.9 0.7 copy.37
  43.6 0.0 all-gather.5.cloned.1.call-update
  43.6 0.0 reduce-scatter.5.cloned.1.call-start
  43.7 0.1 dynamic_slice.10
  43.8 0.1 dynamic_slice.11
  43.9 1.8 convert_element_type.36
  45.6 13.7 %reduce-scatter.3.cloned.1.call-done = f32[512,576]{0,1:T(8,128)} async-done(((f32[512,1152]{0,1:T(8,128)}), f32[512,576]{0,1:T(8,128)}) %reduce-scatter.3.cloned.1.call-update) | async-done | bytes 1179664 | tf_op jit(solution)/shard_map/reduce_scatter | solution.py:228
  59.3 2.0 fusion.24
  61.3 2.5 all-reduce
  63.8 0.2 add_convert_fusion.2
  64.0 0.3 copy.36
  64.3 0.6 reshape.69
  65.0 146.9 %all-gather.5.cloned.1.call-done = bf16[4,576,4096]{1,0,2:T(4,128)(2,1)} async-done(((bf16[4,576,32]{1,0,2:T(4,128)(2,1)}), bf16[4,576,4096]{1,0,2:T(4,128)(2,1)}) %all-gather.5.cloned.1.call-update) | async-done | bytes 18874384 | tf_op jit(solution)/shard_map/all_gather | solution.py:245
  211.9 32.1 %copy.38 = bf16[4,576,4096]{2,1,0:T(8,128)(2,1)} copy(bf16[4,576,4096]{1,0,2:T(4,128)(2,1)} %all-gather.5.cloned.1.call-done) | data formatting | bytes 37748736 | tf_op jit(solution)/shard_map/all_gather | solution.py:245
  244.0 10.5 %fusion.28 = f32[128,4096]{1,0:T(8,128)} fusion(bf16[128,2304]{1,0:T(8,128)(2,1)S(1)} %reshape.69, bf16[2304,4096]{1,0:T(8,128)(2,1)} %bitcast.28), kind=kOutput, calls=%fused_computation.48 | convolution fusion | flops 2415919104 | bytes 21561344 | tf_op jit(solution)/shard_map/dot_general | solution.py:246
  254.5 0.0 reduce-scatter.5.cloned.1.call-update
  254.5 0.0 all-reduce.3.cloned.1.call-start
  255.3 0.1 copy.39
  255.4 0.1 reshape.72
  255.5 12.3 %reduce-scatter.5.cloned.1.call-done = f32[128,2048]{1,0:T(8,128)} async-done(((f32[128,4096]{1,0:T(8,128)}), f32[128,2048]{1,0:T(8,128)}) %reduce-scatter.5.cloned.1.call-update) | async-done | bytes 1048592 | tf_op jit(solution)/shard_map/reduce_scatter | solution.py:251
  267.8 1.5 fusion.14
  269.3 0.9 fusion.15
  270.2 0.0 all-reduce.3.cloned.1.call-update
  270.2 2.7 psum.30
  272.9 0.2 fusion.13.rows_ref
  273.1 103.5 %shard_map.140 = bf16[2048,2048]{1,0:T(8,128)(2,1)} custom-call(bf16[128,2048]{1,0:T(8,128)(2,1)S(1)} %fusion.13.rows_ref, s32[8,128]{1,0:T(8,128)S(1)} %bitcast.27), custom_call_target="tpu_custom_call" | custom-call | tf_op jit(solution)/shard_map/pallas_call | solution.py:175
  376.6 0.0 all-reduce.3.cloned.1.call-done
  376.6 0.9 broadcast_multiply_fusion
  377.5 6.8 %gather_fusion = f32[1024]{0:T(1024)S(1)} fusion(f32[128,128]{1,0:T(8,128)S(1)} %broadcast_multiply_fusion, s32[1024]{0:T(1024)S(1)} %reshape.72), kind=kCustom, calls=%fused_computation | custom fusion | bytes 16384 | tf_op jit(solution)/shard_map/jit(take_along_axis)/gather | solution.py:266
  384.3 0.1 reshape.75
  384.5 0.6 fusion.20
  385.1 8.6 %copy.45 = bf16[1,2048,2048]{2,1,0:T(8,128)(2,1)} copy(bf16[1,2048,2048]{2,1,0:T(8,128)(2,1)} %bitcast.29) | data formatting | bytes 16777216
  (25 shorter events, 0.2 us)
Async XLA Ops:
  8.0 23.4 %copy-start = (bf16[1152,3,288]{0,2,1:T(8,128)(2,1)S(1)}, bf16[1152,3,288]{0,2,1:T(8,128)(2,1)}, u32[]{:S(2)}) copy-start(bf16[1152,3,288]{0,2,1:T(8,128)(2,1)} %param.18) | copy-start | bytes 5971972
  8.0 21.8 %all-gather.3.cloned.1.call-start = ((), (), s32[]{:S(2)}) async-start(), calls=%async_computation.2 | async-start | bytes 1769472 | tf_op jit(solution)/shard_map/all_gather | solution.py:215
  8.7 50.5 %reduce-scatter.3.cloned.1.call-start = ((), (), s32[]{:S(2)}) async-start(), calls=%async_computation.3 | async-start | bytes 3538944 | tf_op jit(solution)/shard_map/reduce_scatter | solution.py:228
  37.7 2.8 copy-start.4
  40.5 2.4 copy-start.7
  40.5 3.2 copy-start.9
  40.5 3.3 copy-start.10
  40.5 3.3 copy-start.3
  42.8 169.1 %all-gather.5.cloned.1.call-start = ((), (), s32[]{:S(2)}) async-start(), calls=%async_computation.4 | async-start | bytes 21135360 | tf_op jit(solution)/shard_map/all_gather | solution.py:245
  43.6 224.2 %reduce-scatter.5.cloned.1.call-start = ((), (), s32[]{:S(2)}) async-start(), calls=%async_computation.5 | async-start | bytes 3145728 | tf_op jit(solution)/shard_map/reduce_scatter | solution.py:251
  244.0 11.3 %copy-start.2 = (s32[128,8]{0,1:T(8,128)S(1)}, s32[128,8]{0,1:T(8,128)}, u32[]{:S(2)}) copy-start(s32[128,8]{0,1:T(8,128)} %param.25) | copy-start | bytes 12292
  254.5 13.4 %copy-start.6 = (bf16[128,2048]{1,0:T(8,128)(2,1)S(1)}, bf16[128,2048]{1,0:T(8,128)(2,1)}, u32[]{:S(2)}) copy-start(bf16[128,2048]{1,0:T(8,128)(2,1)} %param.15) | copy-start | bytes 1572868
  254.5 14.8 %copy-start.5 = (bf16[2048,128]{1,0:T(8,128)(2,1)S(1)}, bf16[2048,128]{1,0:T(8,128)(2,1)}, u32[]{:S(2)}) copy-start(bf16[2048,128]{1,0:T(8,128)(2,1)} %param.24) | copy-start | bytes 1572868
  254.5 14.8 %copy-start.8 = (f32[2048]{0:T(1024)S(1)}, f32[2048]{0:T(1024)}, u32[]{:S(2)}) copy-start(f32[2048]{0:T(1024)} %param.23) | copy-start | bytes 24580
  254.5 122.1 %all-reduce.3.cloned.1.call-start = ((), (), s32[]{:S(2)}) async-start(), calls=%async_computation.6 | async-start | bytes 131072 | tf_op jit(solution)/shard_map/psum | solution.py:262
  385.1 8.6 %copy-start.1 = (bf16[1152,3,288]{0,2,1:T(8,128)(2,1)S(1)}, bf16[1152,3,288]{0,2,1:T(8,128)(2,1)}, u32[]{:S(2)}) copy-start(bf16[1152,3,288]{0,2,1:T(8,128)(2,1)} %param.18) | copy-start | bytes 5971972
Sparse Core Ops, SparseCore 0:
  10.6 19.0 all-gather.2
  42.9 16.3 reduce-scatter.2
  254.6 13.1 reduce-scatter.4
  270.8 29.9 all-reduce.2
Sparse Core Ops, SparseCore 1:
  47.3 164.5 all-gather.4

commit v2 on v0

v2 whole, which is shorter than its diff:
```python
import math

import jax
import jax.numpy as jnp
from jax import lax
from jax.experimental import pallas as pl
from jax.experimental.pallas import tpu as pltpu
from jax.sharding import PartitionSpec as P

MESH = pl.DeviceIdType.MESH
BF16 = jnp.bfloat16
F32 = jnp.float32
NZ = 8
NX = 4
NY = 4
PLANE = NX * NY
SLOTS = 16
ROWS = 128
TOPK = 8
D = 4096
QUARTER = 1024
V = 1152
HALF_V = 576
PATCHES = 512
HEADS = 4
HEAD = 72
BAND = 288
OWN_COLUMNS = 32
EPS = 1e-06
TEXT = 0
IMAGE = 1


def selection(ids, first_expert):
    experts = first_expert + lax.broadcasted_iota(jnp.int32, (PLANE, ROWS), 0)
    count = jnp.zeros((PLANE, ROWS), F32)
    for k in range(TOPK):
        count += (ids[k : k + 1, :] == experts).astype(F32)
    earlier = (
        lax.broadcasted_iota(jnp.int32, (ROWS, ROWS), 0)
        < lax.broadcasted_iota(jnp.int32, (ROWS, ROWS), 1)
    ).astype(BF16)
    before = jnp.dot(count.astype(BF16), earlier, preferred_element_type=F32)
    slot = lax.broadcasted_iota(jnp.int32, (PLANE, SLOTS, ROWS), 1).astype(F32)
    first = before[:, None, :]
    last = (before + count)[:, None, :]
    chosen = (slot >= first) & (slot < last)
    return jnp.where(chosen, 1.0, 0.0).astype(BF16).reshape(PLANE * SLOTS, ROWS)


def fused_kernel(
    image_ref,
    patches_ref,
    text_ref,
    ids_ref,
    norms_ref,
    proj_ref,
    pout_ref,
    merger_ref,
    tgain_ref,
    router_ref,
    text_out,
    image_out,
    gate_ref,
    cols,
    pix,
    normed,
    qs,
    ks,
    vs,
    ctx,
    part_send,
    part_recv,
    merged,
    merged_peer,
    merged_mine,
    acts,
    weights,
    vis_send,
    vis_recv,
    vis,
    vis_all,
    text_peer,
    ids_peer,
    held_ids,
    held,
    stage,
    parts,
    gates,
    send_sems,
    recv_sems,
    acts_recv,
    vis_all_recv,
    out_send,
    out_recv,
):
    dep = lax.axis_index("dep")
    h = lax.axis_index("tp")
    z = dep // PLANE
    xy = lax.rem(dep, PLANE)
    x = xy // NY
    y = lax.rem(xy, NY)
    pair = y // 2
    p = lax.rem(y, 2)
    outs = (text_out, image_out)

    def at(to_z, to_x, to_y):
        return to_z * PLANE + to_x * NY + to_y

    def along_z(step):
        return {"dep": at(lax.rem(z + step, NZ), x, y)}

    def along_x(step):
        return {"dep": at(z, lax.rem(x + step, NX), y)}

    def along_y(step):
        return at(z, x, lax.rem(y + step, NY))

    def in_plane(step):
        to_x = lax.rem(x + step // NY, NX)
        to_y = lax.rem(y + lax.rem(step, NY), NY)
        return to_x * NY + to_y

    other_chip = dep + 1 - 2 * p
    number = [0]

    def remote(source, target, device, arrival=None):
        n = number[0]
        number[0] += 1
        copy = pltpu.make_async_remote_copy(
            src_ref=source,
            dst_ref=target,
            send_sem=send_sems.at[n],
            recv_sem=recv_sems.at[n] if arrival is None else arrival,
            device_id=device,
            device_id_type=MESH,
        )
        copy.start()
        started.append(copy)
        return copy

    started = []

    def flag(shape):
        return jnp.full(shape, image_ref[0], jnp.int32) == 1

    row_from = lax.broadcasted_iota(jnp.int32, (PATCHES, PATCHES), 0)
    row_to = lax.broadcasted_iota(jnp.int32, (PATCHES, PATCHES), 1)
    order = jnp.where(
        row_from == 4 * lax.rem(row_to, ROWS) + row_to // ROWS, 1.0, 0.0
    ).astype(BF16)
    mine = pl.ds(pl.multiple_of(h * HALF_V, HALF_V), HALF_V)
    pix[mine, :] = jnp.dot(patches_ref[...], order, preferred_element_type=F32).astype(BF16)
    weights[:, z, x] = merger_ref[...]

    barrier = pltpu.get_barrier_semaphore()

    def greet(device):
        pl.semaphore_signal(barrier, inc=1, device_id=device, device_id_type=MESH)

    for step in range(1, NZ):
        greet(along_z(step))

    def greet_plane(step, carry):
        greet({"dep": z * PLANE + in_plane(step)})
        return carry

    lax.fori_loop(1, PLANE, greet_plane, 0)
    for step in range(NY):
        greet({"dep": along_y(step), "tp": 1 - h})
    pl.semaphore_wait(barrier, NZ - 1 + PLANE - 1 + NY)

    pix_copy = remote(pix.at[mine], pix.at[mine], {"tp": 1 - h})
    ids_copy = remote(ids_ref, ids_peer, {"dep": other_chip})
    first, second = pl.ds(0, 2), pl.ds(2, 2)
    across_x = [
        remote(merger_ref.at[first], weights.at[first, z, x], along_x(step))
        for step in range(1, NX)
    ]

    def z_hop_a(step):
        back, ahead = lax.rem(z + NZ + 1 - step, NZ), lax.rem(z + step - 1, NZ)
        right = first if step < 4 else pl.ds(0, 1)
        left = first if step < 4 else pl.ds(1, 1)
        return (
            remote(weights.at[right, back], weights.at[right, back], along_z(1)),
            remote(weights.at[left, ahead], weights.at[left, ahead], along_z(NZ - 1)),
        )

    def z_hop_b(step):
        back, ahead = lax.rem(z + NZ + 1 - step, NZ), lax.rem(z + step - 1, NZ)
        right = second if step < 4 else pl.ds(2, 1)
        left = second if step < 4 else pl.ds(3, 1)
        return (
            remote(weights.at[right, back, x], weights.at[right, back, x], along_z(1)),
            remote(weights.at[left, ahead, x], weights.at[left, ahead, x], along_z(NZ - 1)),
        )

    def x_hop_b(step):
        back, ahead = lax.rem(x + NX + 1 - step, NX), lax.rem(x + step - 1, NX)
        right = second if step < 2 else pl.ds(2, 1)
        left = second if step < 2 else pl.ds(3, 1)
        return (
            remote(weights.at[right, :, back], weights.at[right, :, back], along_x(1)),
            remote(weights.at[left, :, ahead], weights.at[left, :, ahead], along_x(NX - 1)),
        )

    def arrived(copies):
        for copy in copies:
            copy.wait_recv()

    hop_b = z_hop_b(1)
    text_columns = pl.ds(pl.multiple_of((1 - p) * QUARTER, QUARTER), QUARTER)
    my_columns = pl.ds(pl.multiple_of(p * QUARTER, QUARTER), QUARTER)
    text_copy = remote(text_ref.at[:, text_columns], text_peer, {"dep": other_chip})

    for v in range(4):
        for c in range(0, V, 128):
            row = jnp.broadcast_to(norms_ref[v : v + 1, c : c + 128], (128, 128))
            cols[v, c : c + 128, :] = row.T

    ids_copy.wait_recv()
    has = flag((TOPK, ROWS))
    held_ids[0, 0:TOPK] = jnp.where(has, ids_peer[...], ids_ref[...])
    held_ids[0, TOPK:] = jnp.where(has, ids_ref[...], ids_peer[...])
    id_copies = [
        remote(held_ids.at[0], held_ids.at[NZ - step], along_z(step)) for step in range(1, NZ)
    ]

    def layer_norm(values, gain, bias):
        mean = jnp.sum(values, 0, keepdims=True) / V
        variance = jnp.sum(values * values, 0, keepdims=True) / V - mean * mean
        return (values - mean) * lax.rsqrt(variance + EPS) * gain + bias

    pix_copy.wait_recv()
    for c in range(0, PATCHES, 128):
        normed[:, c : c + 128] = layer_norm(
            pix[:, c : c + 128].astype(F32), cols[0], cols[1]
        ).astype(BF16)
    pad = jnp.zeros((128 - HEAD, PATCHES), F32)
    queries = jnp.dot(proj_ref[0], normed[...], preferred_element_type=F32)
    for head in range(HEADS):
        part = jnp.concatenate([queries[head * HEAD : (head + 1) * HEAD], pad], 0)
        qs[head] = part.astype(BF16)
    keys = jnp.dot(proj_ref[1], normed[...], preferred_element_type=F32)
    for head in range(HEADS):
        part = jnp.concatenate([keys[head * HEAD : (head + 1) * HEAD], pad], 0)
        ks[head] = part.T.astype(BF16)
    values = jnp.dot(proj_ref[2], normed[...], preferred_element_type=F32)
    for head in range(HEADS):
        vs[head] = values[head * HEAD : (head + 1) * HEAD].astype(BF16)

    arrived(across_x)
    hop_a = z_hop_a(1)
    arrived(hop_b)
    hop_b = z_hop_b(2)

    def start_stats(phase, hidden):
        scaled = hidden * tgain_ref[:, my_columns]
        me = p * 2 + h
        parts[phase, me, :, 0:128] = jnp.dot(
            scaled.astype(BF16), router_ref[p], preferred_element_type=F32
        )
        squares = jnp.sum(hidden * hidden, 1, keepdims=True)
        parts[phase, me, :, 128:256] = jnp.broadcast_to(squares, (ROWS, 128))
        return [
            remote(
                parts.at[phase, me],
                parts.at[phase, me],
                {"dep": dep if dp == 0 else other_chip, "tp": h if dh == 0 else 1 - h},
            )
            for dp, dh in ((0, 1), (1, 0), (1, 1))
        ]

    def normalise(phase, hidden):
        total = parts[phase, 0] + parts[phase, 1] + parts[phase, 2] + parts[phase, 3]
        inv_rms = lax.rsqrt(total[:, 128:129] / D + EPS)
        held[phase, 0] = (hidden * tgain_ref[:, my_columns] * inv_rms).astype(BF16)
        return total

    def gate(phase, total):
        logits = total[:, 0:128].T
        squares = total[:, 128:256].T
        logits = logits * lax.rsqrt(squares[0:1, :] / D + EPS)
        expert = lax.broadcasted_iota(jnp.int32, (128, ROWS), 0)
        ids = held_ids[0, phase * TOPK : (phase + 1) * TOPK]
        for k in range(TOPK):
            gates[phase, k : k + 1, :] = jnp.sum(
                jnp.where(ids[k : k + 1, :] == expert, logits, 0.0), 0, keepdims=True
            )
        chosen = gates[phase]
        raised = jnp.exp(chosen - jnp.max(chosen, 0, keepdims=True))
        return raised / jnp.sum(raised, 0, keepdims=True)

    def ring_hop(phase, step):
        back, ahead = lax.rem(NZ + 1 - step, NZ), step - 1
        right = pl.ds(0, QUARTER if step < 4 else QUARTER // 2)
        left = right if step < 4 else pl.ds(QUARTER // 2, QUARTER // 2)
        return (
            remote(
                held.at[phase, back, :, right], held.at[phase, NZ - step, :, right], along_z(1)
            ),
            remote(
                held.at[phase, ahead, :, left], held.at[phase, step, :, left], along_z(NZ - 1)
            ),
        )

    def spread(phase, slot):
        ids = held_ids[slot, phase * TOPK : (phase + 1) * TOPK]
        chosen = selection(ids, z * PLANE)
        for c in range(0, QUARTER, 512):
            stage[phase, slot, :, c : c + 512] = jnp.dot(
                chosen, held[phase, slot, :, c : c + 512], preferred_element_type=F32
            ).astype(BF16)
        source_pair = lax.rem(z + slot, NZ) * (PLANE // 2) + xy // 2
        at_dest = outs[phase].at[pl.ds(source_pair * SLOTS, SLOTS), my_columns]
        pltpu.make_async_copy(
            stage.at[phase, slot, pl.ds(xy * SLOTS, SLOTS)], at_dest, out_recv.at[phase]
        ).start()

        def send(step, carry):
            peer = in_plane(step)
            pltpu.make_async_remote_copy(
                src_ref=stage.at[phase, slot, pl.ds(peer * SLOTS, SLOTS)],
                dst_ref=at_dest,
                send_sem=out_send.at[phase],
                recv_sem=out_recv.at[phase],
                device_id={"dep": z * PLANE + peer},
                device_id_type=MESH,
            ).start()
            return carry

        lax.fori_loop(1, PLANE, send, 0)

    text_copy.wait_recv()

    def text_hidden():
        return jnp.where(
            flag((ROWS, QUARTER)),
            text_peer[...].astype(F32),
            text_ref[:, my_columns].astype(F32),
        )

    text_stats = start_stats(TEXT, text_hidden())

    def attend(lanes):
        for head in range(HEADS):
            scores = jnp.dot(ks[head], qs[head, :, lanes], preferred_element_type=F32)
            scores = scores * (1.0 / math.sqrt(HEAD))
            raised = jnp.exp(scores - jnp.max(scores, 0, keepdims=True))
            probs = raised * (1.0 / jnp.sum(raised, 0, keepdims=True))
            ctx[head * HEAD : (head + 1) * HEAD, :] = jnp.dot(
                vs[head], probs.astype(BF16), preferred_element_type=F32
            )
        return ctx[...].astype(BF16)

    def out_product(context, lo):
        return lax.dot_general(
            pout_ref[:, lo : lo + 384],
            context,
            (((0,), (0,)), ((), ())),
            preferred_element_type=F32,
        )

    my_rows = pl.ds(pl.multiple_of(h * 256, 256), 256)
    their_rows = pl.ds(pl.multiple_of((1 - h) * 256, 256), 256)
    context = attend(their_rows)
    part_copies = []
    for lo in range(0, V, 384):
        part_send[lo : lo + 384, :] = out_product(context, lo)
        block = pl.ds(lo, 384)
        part_copies.append(remote(part_send.at[block], part_recv.at[block], {"tp": 1 - h}))

    arrived(hop_b)
    hop_b = z_hop_b(3)
    arrived(text_stats)
    text_total = normalise(TEXT, text_hidden())
    ring = ring_hop(TEXT, 1)
    spread(TEXT, 0)

    context = attend(my_rows)
    arrived(hop_b)
    hop_b = z_hop_b(4)
    arrived(hop_a)
    hop_a = z_hop_a(2)
    arrived(part_copies)
    for lo in range(0, V, 384):
        block = pl.ds(lo, 384)
        part_recv[block, :] += out_product(context, lo) + pix[block, my_rows].astype(F32)
    for c in range(0, 256, 128):
        merged[:, c : c + 128] = layer_norm(part_recv[:, c : c + 128], cols[2], cols[3]).astype(
            BF16
        )
    keep = pl.ds(pl.multiple_of(p * 128, 128), 128)
    give = pl.ds(pl.multiple_of((1 - p) * 128, 128), 128)
    merged_copy = remote(merged.at[:, give], merged_peer, {"dep": other_chip})

    arrived(hop_b)
    hop_b = x_hop_b(1)
    arrived(ring)
    ring = ring_hop(TEXT, 2)
    for slot in (1, 7):
        id_copies[NZ - 1 - slot].wait_recv()
        spread(TEXT, slot)
    merged_copy.wait_recv()
    merged_mine[...] = jnp.where(
        flag((V, 128)), merged[:, keep].astype(F32), merged_peer[...].astype(F32)
    ).astype(BF16)
    place = 2 * h + p
    lanes = pl.ds(pl.multiple_of(pair * 128, 128), 128)
    own_half = merged_mine.at[mine]
    theirs = merged_mine.at[pl.ds(pl.multiple_of((1 - h) * HALF_V, HALF_V), HALF_V)]
    pltpu.make_async_copy(own_half, acts.at[place, :, lanes], acts_recv).start()
    for step in range(NY):
        if step > 0:
            remote(own_half, acts.at[place, :, lanes], {"dep": along_y(step)}, acts_recv)
        remote(
            theirs, acts.at[place, :, lanes], {"dep": along_y(step), "tp": 1 - h}, acts_recv
        )

    arrived(hop_a)
    hop_a = z_hop_a(3)
    arrived(ring)
    ring = ring_hop(TEXT, 3)
    for slot in (2, 6):
        id_copies[NZ - 1 - slot].wait_recv()
        spread(TEXT, slot)
    arrived(ring)
    ring = ring_hop(TEXT, 4)
    for slot in (3, 5):
        id_copies[NZ - 1 - slot].wait_recv()
        spread(TEXT, slot)
    arrived(hop_a)
    hop_a = z_hop_a(4)
    arrived(hop_b)
    hop_b = x_hop_b(2)
    arrived(ring)
    id_copies[NZ - 1 - 4].wait_recv()
    spread(TEXT, 4)
    text_gate = gate(TEXT, text_total)
    arrived(hop_a)
    arrived(hop_b)
    pltpu.make_async_copy(acts, acts, acts_recv).wait()

    def columns_of(zs):
        total = None
        for i in range(4):
            block = weights[i, pl.ds(zs, 2)].reshape(2 * NX * OWN_COLUMNS, HALF_V)
            product = jnp.dot(block, acts[i], preferred_element_type=F32)
            total = product if total is None else total + product
        return total

    vis_copies = []
    for c in range(2):
        vis_send[c] = columns_of((1 - h) * 4 + 2 * c)
        vis_copies.append(remote(vis_send.at[c], vis_recv.at[c], {"tp": 1 - h}))
    for c in range(2):
        product = columns_of(h * 4 + 2 * c)
        vis_copies[c].wait_recv()
        vis[pl.ds(8 * c, 8)] = (product + vis_recv[c]).astype(BF16).reshape(8, OWN_COLUMNS, 256)

    def vis_block(to_y):
        return vis.at[
            pl.ds(lax.rem(to_y, 2) * 8, 8), :, pl.ds(pl.multiple_of((to_y // 2) * 128, 128), 128)
        ]

    pltpu.make_async_copy(vis_block(y), vis_all.at[:, y], vis_all_recv).start()
    for step in range(1, NY):
        to_y = lax.rem(y + step, NY)
        remote(vis_block(to_y), vis_all.at[:, y], {"dep": along_y(step)}, vis_all_recv)
    pltpu.make_async_copy(vis_all, vis_all, vis_all_recv).wait()

    def image_hidden():
        return vis_all[...].reshape(QUARTER, ROWS).astype(F32).T

    image_stats = start_stats(IMAGE, image_hidden())
    arrived(image_stats)
    image_total = normalise(IMAGE, image_hidden())
    ring = ring_hop(IMAGE, 1)
    spread(IMAGE, 0)
    image_gate = gate(IMAGE, image_total)
    gate_ref[...] = jnp.where(flag((TOPK, ROWS)), image_gate, text_gate)
    for step in range(1, 5):
        arrived(ring)
        if step < 4:
            ring = ring_hop(IMAGE, step + 1)
        for slot in (step, NZ - step) if step < 4 else (4,):
            spread(IMAGE, slot)

    for copy in started:
        copy.wait_send()
    for phase in (TEXT, IMAGE):
        sent = stage.at[phase, :, pl.ds(0, (PLANE - 1) * SLOTS)]
        pltpu.make_async_copy(sent, sent, out_send.at[phase]).wait()
        pltpu.make_async_copy(outs[phase], outs[phase], out_recv.at[phase]).wait()


def fused(image_count, patches, text, ids, norms, proj, pout, merger, tgain, router):
    vmem = pl.BlockSpec(memory_space=pltpu.VMEM)
    rows = NZ * PLANE // 2 * SLOTS
    buffer = jax.ShapeDtypeStruct((rows, 2 * QUARTER), BF16)
    copies = 96
    return pl.pallas_call(
        fused_kernel,
        out_shape=(buffer, buffer, jax.ShapeDtypeStruct((TOPK, ROWS), F32)),
        in_specs=[pl.BlockSpec(memory_space=pltpu.SMEM)] + [vmem] * 9,
        out_specs=(
            pl.BlockSpec(memory_space=pl.ANY),
            pl.BlockSpec(memory_space=pl.ANY),
            vmem,
        ),
        scratch_shapes=[
            pltpu.VMEM((4, V, 128), F32),
            pltpu.VMEM((V, PATCHES), BF16),
            pltpu.VMEM((V, PATCHES), BF16),
            pltpu.VMEM((HEADS, 128, PATCHES), BF16),
            pltpu.VMEM((HEADS, PATCHES, 128), BF16),
            pltpu.VMEM((HEADS, HEAD, PATCHES), BF16),
            pltpu.VMEM((BAND, 256), F32),
            pltpu.VMEM((V, 256), F32),
            pltpu.VMEM((V, 256), F32),
            pltpu.VMEM((V, 256), BF16),
            pltpu.VMEM((V, 128), BF16),
            pltpu.VMEM((V, 128), BF16),
            pltpu.VMEM((4, HALF_V, 256), BF16),
            pltpu.VMEM((4, NZ, NX, OWN_COLUMNS, HALF_V), BF16),
            pltpu.VMEM((2, 256, 256), F32),
            pltpu.VMEM((2, 256, 256), F32),
            pltpu.VMEM((16, OWN_COLUMNS, 256), BF16),
            pltpu.VMEM((8, NY, OWN_COLUMNS, ROWS), BF16),
            pltpu.VMEM((ROWS, QUARTER), BF16),
            pltpu.VMEM((TOPK, ROWS), jnp.int32),
            pltpu.VMEM((NZ, 2 * TOPK, ROWS), jnp.int32),
            pltpu.VMEM((2, NZ, ROWS, QUARTER), BF16),
            pltpu.VMEM((2, NZ, PLANE * SLOTS, QUARTER), BF16),
            pltpu.VMEM((2, 4, ROWS, 256), F32),
            pltpu.VMEM((2, TOPK, ROWS), F32),
            pltpu.SemaphoreType.DMA((copies,)),
            pltpu.SemaphoreType.DMA((copies,)),
            pltpu.SemaphoreType.DMA,
            pltpu.SemaphoreType.DMA,
            pltpu.SemaphoreType.DMA((2,)),
            pltpu.SemaphoreType.DMA((2,)),
        ],
        compiler_params=pltpu.CompilerParams(
            collective_id=0, has_side_effects=True, vmem_limit_bytes=56 * 1024 * 1024
        ),
    )(image_count, patches, text, ids, norms, proj, pout, merger, tgain, router)


def interleave_kernel(counts_ref, text_ref, image_ref, out_ref, sem):
    def pair_rows(ref, k):
        return ref.at[pl.ds(pl.multiple_of(k * SLOTS, SLOTS), SLOTS)]

    def step(k, carry):
        first = counts_ref[2 * k]
        pltpu.make_async_copy(pair_rows(text_ref, k), pair_rows(out_ref, 2 * k + first), sem).start()
        pltpu.make_async_copy(
            pair_rows(image_ref, k), pair_rows(out_ref, 2 * k + 1 - first), sem
        ).start()
        return carry

    lax.fori_loop(0, counts_ref.shape[0] // 2, step, 0)
    pltpu.make_async_copy(out_ref, out_ref, sem).wait()


def interleave(counts, text_rows, image_rows):
    return pl.pallas_call(
        interleave_kernel,
        out_shape=jax.ShapeDtypeStruct((2 * text_rows.shape[0], text_rows.shape[1]), BF16),
        in_specs=[
            pl.BlockSpec(memory_space=pltpu.SMEM),
            pl.BlockSpec(memory_space=pl.ANY),
            pl.BlockSpec(memory_space=pl.ANY),
        ],
        out_specs=pl.BlockSpec(memory_space=pl.ANY),
        scratch_shapes=[pltpu.SemaphoreType.DMA],
    )(counts, text_rows, image_rows)


def per_device(
    patches,
    image_count,
    text_tokens,
    norm_gain,
    norm_bias,
    patch_proj,
    patch_out,
    merge_gain,
    merge_bias,
    merger,
    token_gain,
    router,
    expert_ids,
):
    counts = lax.all_gather(image_count, "dep", axis=0, tiled=True)
    text_rows, image_rows, gates = fused(
        image_count,
        patches.T,
        text_tokens,
        expert_ids.T,
        jnp.stack([norm_gain, norm_bias, merge_gain, merge_bias]),
        patch_proj.transpose(1, 2, 0),
        patch_out,
        merger.transpose(0, 2, 1),
        token_gain[None],
        router.reshape(2, QUARTER, router.shape[1]),
    )
    return interleave(counts, text_rows, image_rows)[None], gates.T


def solution(mesh):
    return jax.shard_map(
        per_device,
        mesh=mesh,
        in_specs=(
            P("dep", "tp"),
            P("dep"),
            P("dep", "tp"),
            P(),
            P(),
            P(None, None, "tp"),
            P("tp", None),
            P(),
            P(),
            P(None, "tp", "dep"),
            P("tp"),
            P("tp", None),
            P("dep", None),
        ),
        out_specs=(P("dep", None, "tp"), P("dep", None)),
        check_vma=False,
    )
```

time: 515 us -> 457 us (0.89)
  Pallas kernels: 0 us -> 423 us
  waiting for transfers between devices: 368 us -> 0 us
  local copies, waits for them, and re-layouts: 75.5 us -> 5.42 us
  matrix products: 22.4 us -> 0 us
  blocking collectives: 4.94 us -> 26.3 us
  between operations: 16.1 us -> 1.32 us
  starting transfers between devices: 14.6 us -> 0 us
  other arithmetic: 9.54 us -> 0.63 us
    pallas_call x0 -> x2, Pallas kernels: none -> 423 us  [the longest x1 256 us: interleave(): pl.pallas_call(interleave_kernel, out_shape=jax.ShapeDtypeStruct((2 * tex...]
    all_gather x2 -> x0, waiting for transfers between devices: 168 us -> none  [the longest x1 147 us: per_device(): shard_piece = lax.all_gather(merger, 'dep', axis=2, tiled=True)]
    all_to_all x1 -> x0, waiting for transfers between devices: 143 us -> none  [per_device(): lax.all_to_all(outgoing, 'dep', split_axis=0, concat_axis=1, tiled=True)]
    all_gather x1 -> x0, local copies, waits for them, and re-layouts: 32.1 us -> none  [per_device(): shard_piece = lax.all_gather(merger, 'dep', axis=2, tiled=True)]
    psum x1 -> x0, waiting for transfers between devices: 31.8 us -> none  [per_device(): lax.psum((partial_logits, jnp.sum(hidden_f * hidden_f, -1)), 'tp')]
    unnamed x0 -> x1, blocking collectives: none -> 26.3 us
    scatter x1 -> x0, local copies, waits for them, and re-layouts: 25.1 us -> none  [per_device(): buffer = jnp.zeros((expert_count * slot_count, normed.shape[1]), jnp.bflo...]
    reduce_scatter x2 -> x0, waiting for transfers between devices: 24.9 us -> none  [the longest x1 13.7 us: per_device(): lax.psum_scatter(jnp.dot(attended_output, patch_out, preferred_element_ty...]
  transfers between devices with their start and end apart: 6 -> 0, of which waited for: 6 -> 0; matrix products, arithmetic and copies ran while one was open for 3% -> 0% of each run, Pallas kernels for 0% -> 0%
where the time goes in v2:
time: 457 us; the launch traced here: 456 us
  Pallas kernels  423 us (93%)
  blocking collectives  26.3 us (6%)
  local copies, waits for them, and re-layouts  5.42 us (1%)
    pallas_call x1, Pallas kernels, interleave(): pl.pallas_call(interleave_kernel, out_shape=jax.ShapeDtypeStruct((2 * tex...  256 us
    pallas_call x1, Pallas kernels, fused(): pl.pallas_call(fused_kernel, out_shape=(buffer, buffer, jax.ShapeDtypeStr...  167 us
    unnamed x1, blocking collectives  26.3 us

profile of v2, /device:TPU:1, one launch (start us, length us, event | category | flops | bytes accessed | tf_op | source)
XLA Modules:
  0.0 456.1 jit_solution(14605964391682797842)
XLA Ops:
  1.3 1.3 dynamic-slice
  2.5 0.8 dynamic-update-slice
  3.3 26.3 %all-reduce.counts_ref = s32[128]{0:T(128)} all-reduce(s32[128]{0:T(128)S(1)} %dynamic-update-slice), channel_id=1, replica_groups=mesh['dep'=128,'tp'=2] {'dep'}, use_global_device_ids=true, to_apply=%add | all-reduce | flops 128 | bytes 1024
  29.6 0.7 stack.15
  30.3 0.7 stack.16
  31.0 0.7 stack.17
  31.7 0.7 stack.18
  32.4 0.6 pad_maximum_fusion.norms_ref
  33.0 166.6 %shard_map.140 = (bf16[1024,2048]{1,0:T(8,128)(2,1)}, bf16[1024,2048]{1,0:T(8,128)(2,1)}, f32[8,128]{1,0:T(8,128)}) custom-call(s32[1]{0:T(128)S(6)} %copy.17.image_ref, bf16[576,512]{1,0:T(8,128)(2,1)} %bitcast.11, bf16[128,2048]{1,0:T(8,128)(2,1)} %text_ref.1, s32[8,128]{1,0:T(8,128)} %bitcast.15, f32[4,1152]{1,0:T(4,128)} %pad_maximum_fusion.norms_ref, ...), custom_call_target="tpu_custom_call" | custom-call | tf_op jit(solution)/shard_map/pallas_call | solution.py:503
  199.6 0.0 copy-start
  199.6 255.9 %shard_map.141 = bf16[2048,2048]{1,0:T(8,128)(2,1)} custom-call(s32[128]{0:T(128)} %all-reduce.counts_ref, bf16[1024,2048]{1,0:T(8,128)(2,1)} %get-tuple-element.5.text_ref, bf16[1024,2048]{1,0:T(8,128)(2,1)} %get-tuple-element.6.image_ref), custom_call_target="tpu_custom_call" | custom-call | tf_op jit(solution)/shard_map/pallas_call | solution.py:568
  455.5 0.0 copy-done
  455.5 0.6 copy.18
  (1 shorter events, 0.0 us)
Async XLA Ops:
  199.6 255.9 %copy-start = (f32[8,128]{1,0:T(8,128)S(1)}, f32[8,128]{1,0:T(8,128)}, u32[]{:S(2)}) copy-start(f32[8,128]{1,0:T(8,128)} %get-tuple-element.7) | copy-start | bytes 12292

commit v3 on v2

--- a/solution.py
+++ b/solution.py
@@ -53,7 +53,10 @@
     patches_ref,
     text_ref,
     ids_ref,
-    norms_ref,
+    norm_gain_ref,
+    norm_bias_ref,
+    merge_gain_ref,
+    merge_bias_ref,
     proj_ref,
     pout_ref,
     merger_ref,
@@ -62,6 +65,7 @@
     text_out,
     image_out,
     gate_ref,
+    counts_ref,
     cols,
     pix,
     normed,
@@ -83,6 +87,8 @@
     text_peer,
     ids_peer,
     held_ids,
+    plane_counts,
+    all_counts,
     held,
     stage,
     parts,
@@ -93,6 +99,8 @@
     vis_all_recv,
     out_send,
     out_recv,
+    counts_send,
+    counts_recv,
 ):
     dep = lax.axis_index("dep")
     h = lax.axis_index("tp")
@@ -214,15 +222,16 @@
     my_columns = pl.ds(pl.multiple_of(p * QUARTER, QUARTER), QUARTER)
     text_copy = remote(text_ref.at[:, text_columns], text_peer, {"dep": other_chip})
 
-    for v in range(4):
+    for v, vector in enumerate((norm_gain_ref, norm_bias_ref, merge_gain_ref, merge_bias_ref)):
         for c in range(0, V, 128):
-            row = jnp.broadcast_to(norms_ref[v : v + 1, c : c + 128], (128, 128))
+            row = jnp.broadcast_to(vector[c : c + 128].reshape(1, 128), (128, 128))
             cols[v, c : c + 128, :] = row.T
 
     ids_copy.wait_recv()
     has = flag((TOPK, ROWS))
     held_ids[0, 0:TOPK] = jnp.where(has, ids_peer[...], ids_ref[...])
-    held_ids[0, TOPK:] = jnp.where(has, ids_ref[...], ids_peer[...])
+    held_ids[0, TOPK : 2 * TOPK] = jnp.where(has, ids_ref[...], ids_peer[...])
+    held_ids[0, 2 * TOPK :] = jnp.full((8, ROWS), image_ref[0], jnp.int32)
     id_copies = [
         remote(held_ids.at[0], held_ids.at[NZ - step], along_z(step)) for step in range(1, NZ)
     ]
@@ -256,7 +265,7 @@
     hop_b = z_hop_b(2)
 
     def start_stats(phase, hidden):
-        scaled = hidden * tgain_ref[:, my_columns]
+        scaled = hidden * tgain_ref[my_columns].reshape(1, QUARTER)
         me = p * 2 + h
         parts[phase, me, :, 0:128] = jnp.dot(
             scaled.astype(BF16), router_ref[p], preferred_element_type=F32
@@ -275,7 +284,7 @@
     def normalise(phase, hidden):
         total = parts[phase, 0] + parts[phase, 1] + parts[phase, 2] + parts[phase, 3]
         inv_rms = lax.rsqrt(total[:, 128:129] / D + EPS)
-        held[phase, 0] = (hidden * tgain_ref[:, my_columns] * inv_rms).astype(BF16)
+        held[phase, 0] = (hidden * tgain_ref[my_columns].reshape(1, QUARTER) * inv_rms).astype(BF16)
         return total
 
     def gate(phase, total):
@@ -438,6 +447,22 @@
     id_copies[NZ - 1 - 4].wait_recv()
     spread(TEXT, 4)
     text_gate = gate(TEXT, text_total)
+    for slot in range(NZ):
+        plane_counts[pl.ds(lax.rem(z + slot, NZ), 1), :] = held_ids[slot, 2 * TOPK : 2 * TOPK + 1]
+    all_counts[xy] = plane_counts[...]
+
+    def send_counts(step, carry):
+        pltpu.make_async_remote_copy(
+            src_ref=plane_counts,
+            dst_ref=all_counts.at[xy],
+            send_sem=counts_send,
+            recv_sem=counts_recv,
+            device_id={"dep": z * PLANE + in_plane(step)},
+            device_id_type=MESH,
+        ).start()
+        return carry
+
+    lax.fori_loop(1, PLANE, send_counts, 0)
     arrived(hop_a)
     arrived(hop_b)
     pltpu.make_async_copy(acts, acts, acts_recv).wait()
@@ -489,6 +514,14 @@
 
     for copy in started:
         copy.wait_send()
+    others = all_counts.at[pl.ds(0, PLANE - 1)]
+    pltpu.make_async_copy(others, others, counts_send).wait()
+    pltpu.make_async_copy(others, others, counts_recv).wait()
+    lane = lax.broadcasted_iota(jnp.int32, (NZ, ROWS), 1)
+    total_counts = jnp.zeros((NZ, ROWS), jnp.int32)
+    for source in range(PLANE):
+        total_counts += jnp.where(lane == source, all_counts[source], 0)
+    counts_ref[...] = total_counts
     for phase in (TEXT, IMAGE):
         sent = stage.at[phase, :, pl.ds(0, (PLANE - 1) * SLOTS)]
         pltpu.make_async_copy(sent, sent, out_send.at[phase]).wait()
@@ -498,15 +531,21 @@
 def fused(image_count, patches, text, ids, norms, proj, pout, merger, tgain, router):
     vmem = pl.BlockSpec(memory_space=pltpu.VMEM)
     rows = NZ * PLANE // 2 * SLOTS
-    buffer = jax.ShapeDtypeStruct((rows, 2 * QUARTER), BF16)
+    buffer = pltpu.VMEM((rows, 2 * QUARTER), BF16)
     copies = 96
     return pl.pallas_call(
         fused_kernel,
-        out_shape=(buffer, buffer, jax.ShapeDtypeStruct((TOPK, ROWS), F32)),
-        in_specs=[pl.BlockSpec(memory_space=pltpu.SMEM)] + [vmem] * 9,
+        out_shape=(
+            buffer,
+            buffer,
+            jax.ShapeDtypeStruct((TOPK, ROWS), F32),
+            jax.ShapeDtypeStruct((NZ, ROWS), jnp.int32),
+        ),
+        in_specs=[pl.BlockSpec(memory_space=pltpu.SMEM)] + [vmem] * 12,
         out_specs=(
-            pl.BlockSpec(memory_space=pl.ANY),
-            pl.BlockSpec(memory_space=pl.ANY),
+            vmem,
+            vmem,
+            vmem,
             vmem,
         ),
         scratch_shapes=[
@@ -530,7 +569,9 @@
             pltpu.VMEM((8, NY, OWN_COLUMNS, ROWS), BF16),
             pltpu.VMEM((ROWS, QUARTER), BF16),
             pltpu.VMEM((TOPK, ROWS), jnp.int32),
-            pltpu.VMEM((NZ, 2 * TOPK, ROWS), jnp.int32),
+            pltpu.VMEM((NZ, 2 * TOPK + 8, ROWS), jnp.int32),
+            pltpu.VMEM((NZ, ROWS), jnp.int32),
+            pltpu.VMEM((PLANE, NZ, ROWS), jnp.int32),
             pltpu.VMEM((2, NZ, ROWS, QUARTER), BF16),
             pltpu.VMEM((2, NZ, PLANE * SLOTS, QUARTER), BF16),
             pltpu.VMEM((2, 4, ROWS, 256), F32),
@@ -541,11 +582,13 @@
             pltpu.SemaphoreType.DMA,
             pltpu.SemaphoreType.DMA((2,)),
             pltpu.SemaphoreType.DMA((2,)),
+            pltpu.SemaphoreType.DMA,
+            pltpu.SemaphoreType.DMA,
         ],
         compiler_params=pltpu.CompilerParams(
-            collective_id=0, has_side_effects=True, vmem_limit_bytes=56 * 1024 * 1024
+            collective_id=0, has_side_effects=True, vmem_limit_bytes=46 * 1024 * 1024
         ),
-    )(image_count, patches, text, ids, norms, proj, pout, merger, tgain, router)
+    )(image_count, patches, text, ids, *norms, proj, pout, merger, tgain, router)
 
 
 def interleave_kernel(counts_ref, text_ref, image_ref, out_ref, sem):
@@ -553,14 +596,14 @@
         return ref.at[pl.ds(pl.multiple_of(k * SLOTS, SLOTS), SLOTS)]
 
     def step(k, carry):
-        first = counts_ref[2 * k]
+        first = counts_ref[k // (PLANE // 2), 2 * lax.rem(k, PLANE // 2)]
         pltpu.make_async_copy(pair_rows(text_ref, k), pair_rows(out_ref, 2 * k + first), sem).start()
         pltpu.make_async_copy(
             pair_rows(image_ref, k), pair_rows(out_ref, 2 * k + 1 - first), sem
         ).start()
         return carry
 
-    lax.fori_loop(0, counts_ref.shape[0] // 2, step, 0)
+    lax.fori_loop(0, NZ * PLANE // 2, step, 0)
     pltpu.make_async_copy(out_ref, out_ref, sem).wait()
 
 
@@ -570,8 +613,8 @@
         out_shape=jax.ShapeDtypeStruct((2 * text_rows.shape[0], text_rows.shape[1]), BF16),
         in_specs=[
             pl.BlockSpec(memory_space=pltpu.SMEM),
-            pl.BlockSpec(memory_space=pl.ANY),
-            pl.BlockSpec(memory_space=pl.ANY),
+            pl.BlockSpec(memory_space=pltpu.VMEM),
+            pl.BlockSpec(memory_space=pltpu.VMEM),
         ],
         out_specs=pl.BlockSpec(memory_space=pl.ANY),
         scratch_shapes=[pltpu.SemaphoreType.DMA],
@@ -593,17 +636,16 @@
     router,
     expert_ids,
 ):
-    counts = lax.all_gather(image_count, "dep", axis=0, tiled=True)
-    text_rows, image_rows, gates = fused(
+    text_rows, image_rows, gates, counts = fused(
         image_count,
         patches.T,
         text_tokens,
         expert_ids.T,
-        jnp.stack([norm_gain, norm_bias, merge_gain, merge_bias]),
+        (norm_gain, norm_bias, merge_gain, merge_bias),
         patch_proj.transpose(1, 2, 0),
         patch_out,
         merger.transpose(0, 2, 1),
-        token_gain[None],
+        token_gain,
         router.reshape(2, QUARTER, router.shape[1]),
     )
     return interleave(counts, text_rows, image_rows)[None], gates.T

time: 457 us -> 182 us (0.40)
  Pallas kernels: 423 us -> 176 us
  blocking collectives: 26.3 us -> 0 us
    pallas_call x1, Pallas kernels: 256 us -> 6.7 us  [interleave(): pl.pallas_call(interleave_kernel, out_shape=jax.ShapeDtypeStruct((2 * tex...]
    unnamed x1 -> x0, blocking collectives: 26.3 us -> none
where the time goes in v3:
time: 182 us
  Pallas kernels  176 us (97%)
  local copies, waits for them, and re-layouts  4.5 us (2%)
    pallas_call x1, Pallas kernels, fused(): pl.pallas_call(fused_kernel, out_shape=(buffer, buffer, jax.ShapeDtypeStr...  169 us
    pallas_call x1, Pallas kernels, interleave(): pl.pallas_call(interleave_kernel, out_shape=jax.ShapeDtypeStruct((2 * tex...  6.7 us
    unnamed x7, local copies, waits for them, and re-layouts  4.5 us

profile of v3, /device:TPU:1, one launch (start us, length us, event | category | flops | bytes accessed | tf_op | source)
XLA Modules:
  0.0 181.6 jit_solution(11827600832082996168)
XLA Ops:
  1.3 169.1 %shard_map.140 = (bf16[1024,2048]{1,0:T(8,128)(2,1)S(1)}, bf16[1024,2048]{1,0:T(8,128)(2,1)S(1)}, f32[8,128]{1,0:T(8,128)}, s32[8,128]{1,0:T(8,128)}) custom-call(s32[1]{0:T(128)S(6)} %copy.16.image_ref, bf16[576,512]{1,0:T(8,128)(2,1)} %bitcast.9, bf16[128,2048]{1,0:T(8,128)(2,1)} %text_ref.1, s32[8,128]{1,0:T(8,128)} %bitcast.13, f32[1152]{0:T(1024)} %norm_gain_ref.1, ...), custom_call_target="tpu_custom_call" | custom-call | tf_op jit(solution)/shard_map/pallas_call | solution.py:536
  170.4 0.0 copy-start
  170.4 1.9 %copy-done = bf16[1024,2048]{1,0:T(8,128)(2,1)} copy-done((bf16[1024,2048]{1,0:T(8,128)(2,1)}, bf16[1024,2048]{1,0:T(8,128)(2,1)S(1)}, u32[]{:S(2)}) %copy-start) | copy-done | bytes 4194328
  172.3 0.0 copy-start.1
  172.3 2.0 %copy-done.1 = bf16[1024,2048]{1,0:T(8,128)(2,1)} copy-done((bf16[1024,2048]{1,0:T(8,128)(2,1)}, bf16[1024,2048]{1,0:T(8,128)(2,1)S(1)}, u32[]{:S(2)}) %copy-start.1) | copy-done | bytes 4194328
  174.3 0.0 copy-start.2
  174.3 6.7 %shard_map.141 = bf16[2048,2048]{1,0:T(8,128)(2,1)} custom-call(s32[8,128]{1,0:T(8,128)} %get-tuple-element.6.counts_ref, bf16[1024,2048]{1,0:T(8,128)(2,1)} %copy-done, bf16[1024,2048]{1,0:T(8,128)(2,1)} %copy-done.1), custom_call_target="tpu_custom_call" | custom-call | tf_op jit(solution)/shard_map/pallas_call | solution.py:611
  181.0 0.0 copy-done.2
  181.0 0.6 copy.17
Async XLA Ops:
  170.4 1.9 %copy-start = (bf16[1024,2048]{1,0:T(8,128)(2,1)}, bf16[1024,2048]{1,0:T(8,128)(2,1)S(1)}, u32[]{:S(2)}) copy-start(bf16[1024,2048]{1,0:T(8,128)(2,1)S(1)} %get-tuple-element.7.text_ref) | copy-start | bytes 12582916
  172.3 2.0 %copy-start.1 = (bf16[1024,2048]{1,0:T(8,128)(2,1)}, bf16[1024,2048]{1,0:T(8,128)(2,1)S(1)}, u32[]{:S(2)}) copy-start(bf16[1024,2048]{1,0:T(8,128)(2,1)S(1)} %get-tuple-element.8.image_ref) | copy-start | bytes 12582916
  174.3 6.7 %copy-start.2 = (f32[8,128]{1,0:T(8,128)S(1)}, f32[8,128]{1,0:T(8,128)}, u32[]{:S(2)}) copy-start(f32[8,128]{1,0:T(8,128)} %get-tuple-element.9) | copy-start | bytes 12292

commit v4 on v3

v4 whole, which is shorter than its diff:
```python
import math

import jax
import jax.numpy as jnp
from jax import lax
from jax.experimental import pallas as pl
from jax.experimental.pallas import tpu as pltpu
from jax.sharding import PartitionSpec as P

MESH = pl.DeviceIdType.MESH
BF16 = jnp.bfloat16
F32 = jnp.float32
NZ = 8
NX = 4
NY = 4
PLANE = NX * NY
SLOTS = 16
ROWS = 128
TOPK = 8
D = 4096
QUARTER = 1024
V = 1152
HALF_V = 576
PATCHES = 512
HEADS = 4
HEAD = 72
BAND = 288
OWN_COLUMNS = 32
EPS = 1e-06
TEXT = 0
IMAGE = 1


def selection(ids, first_expert):
    experts = first_expert + lax.broadcasted_iota(jnp.int32, (PLANE, ROWS), 0)
    count = jnp.zeros((PLANE, ROWS), F32)
    for k in range(TOPK):
        count += (ids[k : k + 1, :] == experts).astype(F32)
    earlier = (
        lax.broadcasted_iota(jnp.int32, (ROWS, ROWS), 0)
        < lax.broadcasted_iota(jnp.int32, (ROWS, ROWS), 1)
    ).astype(BF16)
    before = jnp.dot(count.astype(BF16), earlier, preferred_element_type=F32)
    slot = lax.broadcasted_iota(jnp.int32, (PLANE, SLOTS, ROWS), 1).astype(F32)
    first = before[:, None, :]
    last = (before + count)[:, None, :]
    chosen = (slot >= first) & (slot < last)
    return jnp.where(chosen, 1.0, 0.0).astype(BF16).reshape(PLANE * SLOTS, ROWS)


def fused_kernel(
    image_ref,
    patches_hbm,
    text_hbm,
    ids_ref,
    norm_gain_ref,
    norm_bias_ref,
    merge_gain_ref,
    merge_bias_ref,
    proj_hbm,
    pout_hbm,
    merger_hbm,
    tgain_ref,
    router_hbm,
    text_out,
    image_out,
    gate_ref,
    counts_ref,
    patches_ref,
    text_ref,
    proj_ref,
    pout_ref,
    merger_ref,
    router_ref,
    cols,
    pix,
    normed,
    qs,
    ks,
    vs,
    ctx,
    part_send,
    part_recv,
    merged,
    merged_peer,
    merged_mine,
    acts,
    weights,
    vis_send,
    vis_recv,
    vis,
    vis_all,
    image_rows,
    text_peer,
    ids_peer,
    held_ids,
    plane_counts,
    all_counts,
    held,
    stage,
    square_parts,
    gate_parts,
    load_sems,
    send_sems,
    recv_sems,
    acts_recv,
    vis_all_recv,
    out_send,
    out_recv,
    counts_send,
    counts_recv,
):
    dep = lax.axis_index("dep")
    h = lax.axis_index("tp")
    z = dep // PLANE
    xy = lax.rem(dep, PLANE)
    x = xy // NY
    y = lax.rem(xy, NY)
    pair = y // 2
    p = lax.rem(y, 2)
    outs = (text_out, image_out)

    def at(to_z, to_x, to_y):
        return to_z * PLANE + to_x * NY + to_y

    def along_z(step):
        return {"dep": at(lax.rem(z + NZ + step, NZ), x, y)}

    def along_x(step):
        return {"dep": at(z, lax.rem(x + NX + step, NX), y)}

    def along_y(step):
        return at(z, x, lax.rem(y + step, NY))

    def in_plane(step):
        mixed = lax.rem(7 * step, PLANE)
        to_x = lax.rem(x + mixed // NY, NX)
        to_y = lax.rem(y + lax.rem(mixed, NY), NY)
        return to_x * NY + to_y

    loads = []
    for n, (source, target) in enumerate(
        (
            (patches_hbm, patches_ref),
            (merger_hbm, merger_ref),
            (text_hbm, text_ref),
            (proj_hbm, proj_ref),
            (router_hbm, router_ref),
            (pout_hbm, pout_ref),
        )
    ):
        load = pltpu.make_async_copy(source, target, load_sems.at[n])
        load.start()
        loads.append(load)

    barrier = pltpu.get_barrier_semaphore()

    def greet(device):
        pl.semaphore_signal(barrier, inc=1, device_id=device, device_id_type=MESH)

    for step in range(1, NZ):
        greet(along_z(step))

    def greet_plane(step, carry):
        greet({"dep": z * PLANE + in_plane(step)})
        return carry

    lax.fori_loop(1, PLANE, greet_plane, 0)
    for step in range(NY):
        greet({"dep": along_y(step), "tp": 1 - h})

    other_chip = dep + 1 - 2 * p
    number = [0]
    started = []

    def remote(source, target, device, arrival=None):
        n = number[0]
        number[0] += 1
        copy = pltpu.make_async_remote_copy(
            src_ref=source,
            dst_ref=target,
            send_sem=send_sems.at[n],
            recv_sem=recv_sems.at[n] if arrival is None else arrival,
            device_id=device,
            device_id_type=MESH,
        )
        copy.start()
        started.append(copy)
        return copy

    def flag(shape):
        return jnp.full(shape, image_ref[0], jnp.int32) == 1

    row_from = lax.broadcasted_iota(jnp.int32, (PATCHES, PATCHES), 0)
    row_to = lax.broadcasted_iota(jnp.int32, (PATCHES, PATCHES), 1)
    order = jnp.where(
        row_from == 4 * lax.rem(row_to, ROWS) + row_to // ROWS, 1.0, 0.0
    ).astype(BF16)
    mine = pl.ds(pl.multiple_of(h * HALF_V, HALF_V), HALF_V)
    loads[0].wait()
    pix[mine, :] = jnp.dot(patches_ref[...], order, preferred_element_type=F32).astype(BF16)
    loads[1].wait()
    for j in range(2):
        weights[j, z, x] = jnp.concatenate([merger_ref[2 * j], merger_ref[2 * j + 1]], 1)
    loads[2].wait()

    pl.semaphore_wait(barrier, NZ - 1 + PLANE - 1 + NY)

    text_columns = pl.ds(pl.multiple_of((1 - p) * QUARTER, QUARTER), QUARTER)
    my_columns = pl.ds(pl.multiple_of(p * QUARTER, QUARTER), QUARTER)
    pix_copy = remote(pix.at[mine], pix.at[mine], {"tp": 1 - h})
    ids_copy = remote(ids_ref, ids_peer, {"dep": other_chip})
    text_copy = remote(text_ref.at[:, text_columns], text_peer, {"dep": other_chip})
    across_x = [
        remote(weights.at[0, z, x], weights.at[0, z, x], along_x(step)) for step in (1, 3, 2)
    ]

    def both_ways(right, left, along):
        return (
            remote(right, right, along(1)),
            remote(left, left, along(-1)),
        )

    def z_hop_a(step):
        back, ahead = lax.rem(z + NZ + 1 - step, NZ), lax.rem(z + step - 1, NZ)
        right = pl.ds(0, 4 if step < 4 else 2)
        left = right if step < 4 else pl.ds(2, 2)
        return both_ways(weights.at[0, back, right], weights.at[0, ahead, left], along_z)

    def z_hop_b(step):
        back, ahead = lax.rem(z + NZ + 1 - step, NZ), lax.rem(z + step - 1, NZ)
        right = pl.ds(0, OWN_COLUMNS if step < 4 else OWN_COLUMNS // 2)
        left = right if step < 4 else pl.ds(OWN_COLUMNS // 2, OWN_COLUMNS // 2)
        return both_ways(weights.at[1, back, x, right], weights.at[1, ahead, x, left], along_z)

    def x_hop_b(step):
        back, ahead = lax.rem(x + NX + 1 - step, NX), lax.rem(x + step - 1, NX)
        right = pl.ds(0, NZ if step < 2 else NZ // 2)
        left = right if step < 2 else pl.ds(NZ // 2, NZ // 2)
        return both_ways(weights.at[1, right, back], weights.at[1, left, ahead], along_x)

    def arrived(copies):
        for copy in copies:
            copy.wait_recv()

    hop_b = z_hop_b(1)

    for v, vector in enumerate((norm_gain_ref, norm_bias_ref, merge_gain_ref, merge_bias_ref)):
        for c in range(0, V, 128):
            row = jnp.broadcast_to(vector[c : c + 128].reshape(1, 128), (128, 128))
            cols[v, c : c + 128, :] = row.T

    def layer_norm(values, gain, bias):
        mean = jnp.sum(values, 0, keepdims=True) / V
        variance = jnp.sum(values * values, 0, keepdims=True) / V - mean * mean
        return (values - mean) * lax.rsqrt(variance + EPS) * gain + bias

    def to_unit(parts, phase):
        me = p * 2 + h
        return [
            remote(
                parts.at[phase, me],
                parts.at[phase, me],
                {"dep": dep if dp == 0 else other_chip, "tp": h if dh == 0 else 1 - h},
            )
            for dp, dh in ((0, 1), (1, 0), (1, 1))
        ]

    def total_of(parts, phase):
        return parts[phase, 0] + parts[phase, 1] + parts[phase, 2] + parts[phase, 3]

    def inv_rms(phase):
        return lax.rsqrt(total_of(square_parts, phase)[0:1, :] / D + EPS)

    def start_squares(phase, squares):
        square_parts[phase, p * 2 + h] = jnp.broadcast_to(squares, (8, ROWS))
        return to_unit(square_parts, phase)

    def start_gates(phase, hidden):
        scaled = hidden * tgain_ref[my_columns].reshape(1, QUARTER)
        logits = jnp.dot(scaled.astype(BF16), router_ref[p], preferred_element_type=F32).T
        expert = lax.broadcasted_iota(jnp.int32, (128, ROWS), 0)
        ids = held_ids[0, phase * TOPK : (phase + 1) * TOPK]
        me = p * 2 + h
        for k in range(TOPK):
            gate_parts[phase, me, k : k + 1, :] = jnp.sum(
                jnp.where(ids[k : k + 1, :] == expert, logits, 0.0), 0, keepdims=True
            )
        return to_unit(gate_parts, phase)

    def normalise(phase, hidden):
        inverse = jnp.broadcast_to(inv_rms(phase), (ROWS, ROWS)).T[:, 0:1]
        held[phase, 0] = (hidden * tgain_ref[my_columns].reshape(1, QUARTER) * inverse).astype(BF16)

    def gate(phase):
        chosen = total_of(gate_parts, phase) * inv_rms(phase)
        raised = jnp.exp(chosen - jnp.max(chosen, 0, keepdims=True))
        return raised / jnp.sum(raised, 0, keepdims=True)

    def ring_hop(phase, step):
        back, ahead = lax.rem(NZ + 1 - step, NZ), step - 1
        right = pl.ds(0, QUARTER if step < 4 else QUARTER // 2)
        left = right if step < 4 else pl.ds(QUARTER // 2, QUARTER // 2)
        return (
            remote(
                held.at[phase, back, :, right], held.at[phase, NZ - step, :, right], along_z(1)
            ),
            remote(
                held.at[phase, ahead, :, left], held.at[phase, step, :, left], along_z(NZ - 1)
            ),
        )

    def spread(phase, slot):
        ids = held_ids[slot, phase * TOPK : (phase + 1) * TOPK]
        chosen = selection(ids, z * PLANE)
        for c in range(0, QUARTER, 512):
            stage[phase, slot, :, c : c + 512] = jnp.dot(
                chosen, held[phase, slot, :, c : c + 512], preferred_element_type=F32
            ).astype(BF16)
        source_pair = lax.rem(z + slot, NZ) * (PLANE // 2) + xy // 2
        at_dest = outs[phase].at[pl.ds(source_pair * SLOTS, SLOTS), my_columns]
        pltpu.make_async_copy(
            stage.at[phase, slot, pl.ds(xy * SLOTS, SLOTS)], at_dest, out_recv.at[phase]
        ).start()

        def send(step, carry):
            peer = in_plane(step)
            pltpu.make_async_remote_copy(
                src_ref=stage.at[phase, slot, pl.ds(peer * SLOTS, SLOTS)],
                dst_ref=at_dest,
                send_sem=out_send.at[phase],
                recv_sem=out_recv.at[phase],
                device_id={"dep": z * PLANE + peer},
                device_id_type=MESH,
            ).start()
            return carry

        lax.fori_loop(1, PLANE, send, 0)

    def text_hidden():
        return jnp.where(
            flag((ROWS, QUARTER)),
            text_peer[...].astype(F32),
            text_ref[:, my_columns].astype(F32),
        )

    def text_spread(*slots):
        for slot in slots:
            if slot:
                id_copies[NZ - 1 - slot].wait_recv()
            spread(TEXT, slot)

    def attend(lanes):
        for head in range(HEADS):
            scores = jnp.dot(ks[head], qs[head, :, lanes], preferred_element_type=F32)
            below = scores - jnp.max(scores, 0, keepdims=True)
            raised = jnp.exp2(below * (math.log2(math.e) / math.sqrt(HEAD))).astype(BF16)
            product = jnp.dot(vs[head], raised, preferred_element_type=F32)
            ctx[head * HEAD : (head + 1) * HEAD, :] = product[:HEAD] / product[HEAD : HEAD + 1]
        return ctx[...].astype(BF16)

    def out_product(context, lo):
        return lax.dot_general(
            pout_ref[:, lo : lo + 384],
            context,
            (((0,), (0,)), ((), ())),
            preferred_element_type=F32,
        )

    pix_copy.wait_recv()
    for c in range(0, PATCHES, 128):
        normed[:, c : c + 128] = layer_norm(
            pix[:, c : c + 128].astype(F32), cols[0], cols[1]
        ).astype(BF16)
    loads[3].wait()
    pad = jnp.zeros((128 - HEAD, PATCHES), F32)
    queries = jnp.dot(proj_ref[0], normed[...], preferred_element_type=F32)
    for head in range(HEADS):
        part = jnp.concatenate([queries[head * HEAD : (head + 1) * HEAD], pad], 0)
        qs[head] = part.astype(BF16)
    keys = jnp.dot(proj_ref[1], normed[...], preferred_element_type=F32)
    for head in range(HEADS):
        part = jnp.concatenate([keys[head * HEAD : (head + 1) * HEAD], pad], 0)
        ks[head] = part.T.astype(BF16)
    values = jnp.dot(proj_ref[2], normed[...], preferred_element_type=F32)
    ones = jnp.ones((8, PATCHES), F32)
    for head in range(HEADS):
        part = jnp.concatenate([values[head * HEAD : (head + 1) * HEAD], ones], 0)
        vs[head] = part.astype(BF16)

    ids_copy.wait_recv()
    has = flag((TOPK, ROWS))
    held_ids[0, 0:TOPK] = jnp.where(has, ids_peer[...], ids_ref[...])
    held_ids[0, TOPK : 2 * TOPK] = jnp.where(has, ids_ref[...], ids_peer[...])
    held_ids[0, 2 * TOPK :] = jnp.full((8, ROWS), image_ref[0], jnp.int32)
    id_copies = [
        remote(held_ids.at[0], held_ids.at[NZ - step], along_z(step)) for step in range(1, NZ)
    ]

    my_rows = pl.ds(pl.multiple_of(h * 256, 256), 256)
    their_rows = pl.ds(pl.multiple_of((1 - h) * 256, 256), 256)
    context = attend(their_rows)
    loads[5].wait()
    part_copies = []
    for lo in range(0, V, 384):
        part_send[lo : lo + 384, :] = out_product(context, lo)
        block = pl.ds(lo, 384)
        part_copies.append(remote(part_send.at[block], part_recv.at[block], {"tp": 1 - h}))
    arrived(hop_b)
    hop_b = z_hop_b(2)
    arrived(across_x)
    hop_a = z_hop_a(1)
    context = attend(my_rows)
    text_copy.wait_recv()
    hidden = text_hidden()
    squares = jnp.broadcast_to(jnp.sum(hidden * hidden, 1, keepdims=True), (ROWS, ROWS))
    text_squares = start_squares(TEXT, squares.T[0:1, :])
    arrived(part_copies)
    for lo in range(0, V, 384):
        block = pl.ds(lo, 384)
        part_recv[block, :] += out_product(context, lo) + pix[block, my_rows].astype(F32)
    for c in range(0, 256, 128):
        merged[:, c : c + 128] = layer_norm(part_recv[:, c : c + 128], cols[2], cols[3]).astype(
            BF16
        )
    keep = pl.ds(pl.multiple_of(p * 128, 128), 128)
    give = pl.ds(pl.multiple_of((1 - p) * 128, 128), 128)
    merged_copy = remote(merged.at[:, give], merged_peer, {"dep": other_chip})

    arrived(text_squares)
    normalise(TEXT, text_hidden())
    ring = ring_hop(TEXT, 1)
    text_spread(0)
    arrived(hop_b)
    hop_b = z_hop_b(3)
    arrived(hop_a)
    hop_a = z_hop_a(2)
    merged_copy.wait_recv()
    merged_mine[...] = jnp.where(
        flag((V, 128)), merged[:, keep].astype(F32), merged_peer[...].astype(F32)
    ).astype(BF16)
    lanes = pl.ds(pl.multiple_of(pair * 128, 128), 128)
    own_half = merged_mine.at[mine]
    theirs = merged_mine.at[pl.ds(pl.multiple_of((1 - h) * HALF_V, HALF_V), HALF_V)]
    place = acts.at[h, pl.ds(pl.multiple_of(p * HALF_V, HALF_V), HALF_V), lanes]
    pltpu.make_async_copy(own_half, place, acts_recv).start()
    for step in (1, 3, 2, 0):
        if step > 0:
            remote(own_half, place, {"dep": along_y(step)}, acts_recv)
        remote(theirs, place, {"dep": along_y(step), "tp": 1 - h}, acts_recv)
    arrived(hop_b)
    hop_b = z_hop_b(4)
    arrived(ring)
    ring = ring_hop(TEXT, 2)
    text_spread(1, 7)
    arrived(hop_b)
    hop_b = x_hop_b(1)
    arrived(hop_a)
    hop_a = z_hop_a(3)
    arrived(ring)
    ring = ring_hop(TEXT, 3)
    text_spread(2, 6)
    arrived(hop_a)
    hop_a = z_hop_a(4)
    arrived(hop_b)
    hop_b = x_hop_b(2)
    arrived(ring)
    ring = ring_hop(TEXT, 4)
    text_spread(3, 5)
    arrived(ring)
    text_spread(4)
    loads[4].wait()
    text_gates = start_gates(TEXT, text_hidden())
    for slot in range(NZ):
        plane_counts[pl.ds(lax.rem(z + slot, NZ), 1), :] = held_ids[slot, 2 * TOPK : 2 * TOPK + 1]
    all_counts[xy] = plane_counts[...]

    def send_counts(step, carry):
        pltpu.make_async_remote_copy(
            src_ref=plane_counts,
            dst_ref=all_counts.at[xy],
            send_sem=counts_send,
            recv_sem=counts_recv,
            device_id={"dep": z * PLANE + in_plane(step)},
            device_id_type=MESH,
        ).start()
        return carry

    lax.fori_loop(1, PLANE, send_counts, 0)
    arrived(hop_a)
    arrived(hop_b)
    pltpu.make_async_copy(acts, acts, acts_recv).wait()

    def columns_of(zs):
        total = None
        for j in range(2):
            block = weights[j, pl.ds(zs, 2)].reshape(2 * NX * OWN_COLUMNS, V)
            product = jnp.dot(block, acts[j], preferred_element_type=F32)
            total = product if total is None else total + product
        return total

    vis_copies = []
    for c in range(2):
        vis_send[c] = columns_of((1 - h) * 4 + 2 * c)
        vis_copies.append(remote(vis_send.at[c], vis_recv.at[c], {"tp": 1 - h}))
    for c in range(2):
        product = columns_of(h * 4 + 2 * c)
        vis_copies[c].wait_recv()
        vis[pl.ds(8 * c, 8)] = (product + vis_recv[c]).astype(BF16).reshape(8, OWN_COLUMNS, 256)

    def vis_block(to_y):
        return vis.at[
            pl.ds(lax.rem(to_y, 2) * 8, 8), :, pl.ds(pl.multiple_of((to_y // 2) * 128, 128), 128)
        ]

    pltpu.make_async_copy(vis_block(y), vis_all.at[:, y], vis_all_recv).start()
    for step in range(1, NY):
        to_y = lax.rem(y + step, NY)
        remote(vis_block(to_y), vis_all.at[:, y], {"dep": along_y(step)}, vis_all_recv)
    pltpu.make_async_copy(vis_all, vis_all, vis_all_recv).wait()

    hidden = vis_all[...].reshape(QUARTER, ROWS).astype(F32)
    image_squares = start_squares(IMAGE, jnp.sum(hidden * hidden, 0, keepdims=True))
    image_rows[...] = hidden.T
    arrived(image_squares)
    normalise(IMAGE, image_rows[...])
    ring = ring_hop(IMAGE, 1)
    spread(IMAGE, 0)
    image_gates = start_gates(IMAGE, image_rows[...])
    for step in range(1, 5):
        arrived(ring)
        if step < 4:
            ring = ring_hop(IMAGE, step + 1)
        for slot in (step, NZ - step) if step < 4 else (4,):
            spread(IMAGE, slot)
    arrived(text_gates)
    arrived(image_gates)
    gate_ref[...] = jnp.where(flag((TOPK, ROWS)), gate(IMAGE), gate(TEXT))

    for copy in started:
        copy.wait_send()
    others = all_counts.at[pl.ds(0, PLANE - 1)]
    pltpu.make_async_copy(others, others, counts_send).wait()
    pltpu.make_async_copy(others, others, counts_recv).wait()
    lane = lax.broadcasted_iota(jnp.int32, (NZ, ROWS), 1)
    total_counts = jnp.zeros((NZ, ROWS), jnp.int32)
    for source in range(PLANE):
        total_counts += jnp.where(lane == source, all_counts[source], 0)
    counts_ref[...] = total_counts
    for phase in (TEXT, IMAGE):
        sent = stage.at[phase, :, pl.ds(0, (PLANE - 1) * SLOTS)]
        pltpu.make_async_copy(sent, sent, out_send.at[phase]).wait()
        pltpu.make_async_copy(outs[phase], outs[phase], out_recv.at[phase]).wait()


def fused(image_count, patches, text, ids, norms, proj, pout, merger, tgain, router):
    vmem = pl.BlockSpec(memory_space=pltpu.VMEM)
    hbm = pl.BlockSpec(memory_space=pl.ANY)
    loaded = (patches, text, proj, pout, merger, router)
    rows = NZ * PLANE // 2 * SLOTS
    buffer = pltpu.VMEM((rows, 2 * QUARTER), BF16)
    copies = 96
    return pl.pallas_call(
        fused_kernel,
        out_shape=(
            buffer,
            buffer,
            pltpu.VMEM((TOPK, ROWS), F32),
            pltpu.VMEM((NZ, ROWS), jnp.int32),
        ),
        in_specs=[pl.BlockSpec(memory_space=pltpu.SMEM), hbm, hbm]
        + [vmem] * 5
        + [hbm] * 3
        + [vmem, hbm],
        out_specs=(
            vmem,
            vmem,
            vmem,
            vmem,
        ),
        scratch_shapes=[pltpu.VMEM(a.shape, a.dtype) for a in loaded]
        + [
            pltpu.VMEM((4, V, 128), F32),
            pltpu.VMEM((V, PATCHES), BF16),
            pltpu.VMEM((V, PATCHES), BF16),
            pltpu.VMEM((HEADS, 128, PATCHES), BF16),
            pltpu.VMEM((HEADS, PATCHES, 128), BF16),
            pltpu.VMEM((HEADS, HEAD + 8, PATCHES), BF16),
            pltpu.VMEM((BAND, 256), F32),
            pltpu.VMEM((V, 256), F32),
            pltpu.VMEM((V, 256), F32),
            pltpu.VMEM((V, 256), BF16),
            pltpu.VMEM((V, 128), BF16),
            pltpu.VMEM((V, 128), BF16),
            pltpu.VMEM((2, V, 256), BF16),
            pltpu.VMEM((2, NZ, NX, OWN_COLUMNS, V), BF16),
            pltpu.VMEM((2, 256, 256), F32),
            pltpu.VMEM((2, 256, 256), F32),
            pltpu.VMEM((16, OWN_COLUMNS, 256), BF16),
            pltpu.VMEM((8, NY, OWN_COLUMNS, ROWS), BF16),
            pltpu.VMEM((ROWS, QUARTER), F32),
            pltpu.VMEM((ROWS, QUARTER), BF16),
            pltpu.VMEM((TOPK, ROWS), jnp.int32),
            pltpu.VMEM((NZ, 2 * TOPK + 8, ROWS), jnp.int32),
            pltpu.VMEM((NZ, ROWS), jnp.int32),
            pltpu.VMEM((PLANE, NZ, ROWS), jnp.int32),
            pltpu.VMEM((2, NZ, ROWS, QUARTER), BF16),
            pltpu.VMEM((2, NZ, PLANE * SLOTS, QUARTER), BF16),
            pltpu.VMEM((2, 4, 8, ROWS), F32),
            pltpu.VMEM((2, 4, TOPK, ROWS), F32),
            pltpu.SemaphoreType.DMA((6,)),
            pltpu.SemaphoreType.DMA((copies,)),
            pltpu.SemaphoreType.DMA((copies,)),
            pltpu.SemaphoreType.DMA,
            pltpu.SemaphoreType.DMA,
            pltpu.SemaphoreType.DMA((2,)),
            pltpu.SemaphoreType.DMA((2,)),
            pltpu.SemaphoreType.DMA,
            pltpu.SemaphoreType.DMA,
        ],
        compiler_params=pltpu.CompilerParams(
            collective_id=0, has_side_effects=True, vmem_limit_bytes=46 * 1024 * 1024
        ),
    )(image_count, patches, text, ids, *norms, proj, pout, merger, tgain, router)


def interleave_kernel(counts_ref, text_ref, image_ref, gate_ref, out_ref, gate_out, sem):
    def pair_rows(ref, k):
        return ref.at[pl.ds(pl.multiple_of(k * SLOTS, SLOTS), SLOTS)]

    def step(k, carry):
        first = counts_ref[k // (PLANE // 2), 2 * lax.rem(k, PLANE // 2)]
        pltpu.make_async_copy(pair_rows(text_ref, k), pair_rows(out_ref, 2 * k + first), sem).start(
            priority=0
        )
        pltpu.make_async_copy(
            pair_rows(image_ref, k), pair_rows(out_ref, 2 * k + 1 - first), sem
        ).start(priority=1)
        return carry

    lax.fori_loop(0, NZ * PLANE // 2, step, 0)
    gate_out[...] = gate_ref[...]
    pltpu.make_async_copy(out_ref, out_ref, sem).wait()


def interleave(counts, text_rows, image_rows, gates):
    vmem = pl.BlockSpec(memory_space=pltpu.VMEM)
    held = pl.BlockSpec(memory_space=pl.ANY)
    return pl.pallas_call(
        interleave_kernel,
        out_shape=(
            jax.ShapeDtypeStruct((2 * text_rows.shape[0], text_rows.shape[1]), BF16),
            jax.ShapeDtypeStruct(gates.shape, F32),
        ),
        in_specs=[pl.BlockSpec(memory_space=pltpu.SMEM), held, held, vmem],
        out_specs=(held, vmem),
        scratch_shapes=[pltpu.SemaphoreType.DMA],
        compiler_params=pltpu.CompilerParams(vmem_limit_bytes=4 * 1024 * 1024),
    )(counts, text_rows, image_rows, gates)


def per_device(
    patches,
    image_count,
    text_tokens,
    norm_gain,
    norm_bias,
    patch_proj,
    patch_out,
    merge_gain,
    merge_bias,
    merger,
    token_gain,
    router,
    expert_ids,
):
    text_rows, image_rows, gates, counts = fused(
        image_count,
        patches.T,
        text_tokens,
        expert_ids.T,
        (norm_gain, norm_bias, merge_gain, merge_bias),
        patch_proj.transpose(1, 2, 0),
        patch_out,
        merger.transpose(0, 2, 1),
        token_gain,
        router.reshape(2, QUARTER, router.shape[1]),
    )
    dispatched, gate_probs = interleave(counts, text_rows, image_rows, gates)
    return dispatched[None], gate_probs.T


def solution(mesh):
    return jax.shard_map(
        per_device,
        mesh=mesh,
        in_specs=(
            P("dep", "tp"),
            P("dep"),
            P("dep", "tp"),
            P(),
            P(),
            P(None, None, "tp"),
            P("tp", None),
            P(),
            P(),
            P(None, "tp", "dep"),
            P("tp"),
            P("tp", None),
            P("dep", None),
        ),
        out_specs=(P("dep", None, "tp"), P("dep", None)),
        check_vma=False,
    )
```

time: 182 us -> 159 us (0.87)
  Pallas kernels: 176 us -> 157 us
  local copies, waits for them, and re-layouts: 4.5 us -> 0 us
    pallas_call x2, Pallas kernels: 176 us -> 157 us  [the longest x1 153 us: fused(): pl.pallas_call(fused_kernel, out_shape=(buffer, buffer, pltpu.VMEM((TOPK,...]
    unnamed x7 -> x0, local copies, waits for them, and re-layouts: 4.5 us -> none
where the time goes in v4:
time: 159 us; the launch traced here: 158 us
  Pallas kernels  157 us (99%)
    pallas_call x1, Pallas kernels, fused(): pl.pallas_call(fused_kernel, out_shape=(buffer, buffer, pltpu.VMEM((TOPK,...  153 us
    pallas_call x1, Pallas kernels, interleave(): pl.pallas_call(interleave_kernel, out_shape=(jax.ShapeDtypeStruct((2 * te...  4.42 us

profile of v4, /device:TPU:1, one launch (start us, length us, event | category | flops | bytes accessed | tf_op | source)
XLA Modules:
  0.0 158.4 jit_solution(5956657562417198552)
XLA Ops:
  1.3 152.7 %shard_map.140 = (bf16[1024,2048]{1,0:T(8,128)(2,1)S(1)}, bf16[1024,2048]{1,0:T(8,128)(2,1)S(1)}, f32[8,128]{1,0:T(8,128)S(1)}, s32[8,128]{1,0:T(8,128)S(1)}) custom-call(s32[1]{0:T(128)S(6)} %copy.15.image_ref, bf16[576,512]{1,0:T(8,128)(2,1)} %bitcast.8, bf16[128,2048]{1,0:T(8,128)(2,1)} %text_hbm.1, s32[8,128]{1,0:T(8,128)} %bitcast.11, ...), custom_call_target="tpu_custom_call" | custom-call | tf_op jit(solution)/shard_map/pallas_call | solution.py:563
  154.0 4.4 %shard_map.141 = (bf16[2048,2048]{1,0:T(8,128)(2,1)}, f32[8,128]{1,0:T(8,128)}) custom-call(s32[8,128]{1,0:T(8,128)S(1)} %get-tuple-element.8.counts_ref, bf16[1024,2048]{1,0:T(8,128)(2,1)S(1)} %get-tuple-element.9.text_ref, bf16[1024,2048]{1,0:T(8,128)(2,1)S(1)} %get-tuple-element.10.image_ref, f32[8,128]{1,0:T(8,128)S(1)} %get-tuple-element.11.gate_ref), custom_call_target="tpu_custom_call" | custom-call | tf_op jit(solution)/shard_map/pallas_call | solution.py:649

commit v5 on v4

--- a/solution.py
+++ b/solution.py
@@ -92,6 +92,9 @@
     vis_all,
     image_rows,
     text_peer,
+    text_normed,
+    text_squares,
+    text_chosen,
     ids_peer,
     held_ids,
     plane_counts,
@@ -203,14 +206,17 @@
     for j in range(2):
         weights[j, z, x] = jnp.concatenate([merger_ref[2 * j], merger_ref[2 * j + 1]], 1)
     loads[2].wait()
+    raw = text_ref[...].astype(F32)
+    squares = jnp.broadcast_to(jnp.sum(raw * raw, 1, keepdims=True), (ROWS, ROWS))
+    text_squares[h] = jnp.broadcast_to(squares.T[0:1, :], (8, ROWS))
 
     pl.semaphore_wait(barrier, NZ - 1 + PLANE - 1 + NY)
 
     text_columns = pl.ds(pl.multiple_of((1 - p) * QUARTER, QUARTER), QUARTER)
     my_columns = pl.ds(pl.multiple_of(p * QUARTER, QUARTER), QUARTER)
+    squares_copy = remote(text_squares.at[h], text_squares.at[h], {"tp": 1 - h})
     pix_copy = remote(pix.at[mine], pix.at[mine], {"tp": 1 - h})
     ids_copy = remote(ids_ref, ids_peer, {"dep": other_chip})
-    text_copy = remote(text_ref.at[:, text_columns], text_peer, {"dep": other_chip})
     across_x = [
         remote(weights.at[0, z, x], weights.at[0, z, x], along_x(step)) for step in (1, 3, 2)
     ]
@@ -233,17 +239,27 @@
         left = right if step < 4 else pl.ds(OWN_COLUMNS // 2, OWN_COLUMNS // 2)
         return both_ways(weights.at[1, back, x, right], weights.at[1, ahead, x, left], along_z)
 
-    def x_hop_b(step):
-        back, ahead = lax.rem(x + NX + 1 - step, NX), lax.rem(x + step - 1, NX)
-        right = pl.ds(0, NZ if step < 2 else NZ // 2)
-        left = right if step < 2 else pl.ds(NZ // 2, NZ // 2)
-        return both_ways(weights.at[1, right, back], weights.at[1, left, ahead], along_x)
-
     def arrived(copies):
         for copy in copies:
             copy.wait_recv()
 
+    def x_send_b(*blocks):
+        for block in blocks:
+            to_share = weights.at[1, lax.rem(z + NZ + block, NZ), x]
+            for step in (1, 3, 2):
+                shared.append(remote(to_share, to_share, along_x(step)))
+
+    shared = []
     hop_b = z_hop_b(1)
+    x_send_b(0)
+
+    squares_copy.wait_recv()
+    text_inverse = lax.rsqrt((text_squares[0] + text_squares[1]) / D + EPS)[0:1, :]
+    inverse = jnp.broadcast_to(text_inverse, (ROWS, ROWS)).T[:, 0:1]
+    text_normed[...] = (
+        text_ref[...].astype(F32) * tgain_ref[...].reshape(1, 2 * QUARTER) * inverse
+    ).astype(BF16)
+    text_copy = remote(text_normed.at[:, text_columns], text_peer, {"dep": other_chip})
 
     for v, vector in enumerate((norm_gain_ref, norm_bias_ref, merge_gain_ref, merge_bias_ref)):
         for c in range(0, V, 128):
@@ -255,45 +271,32 @@
         variance = jnp.sum(values * values, 0, keepdims=True) / V - mean * mean
         return (values - mean) * lax.rsqrt(variance + EPS) * gain + bias
 
-    def to_unit(parts, phase):
+    def to_unit(parts):
         me = p * 2 + h
         return [
             remote(
-                parts.at[phase, me],
-                parts.at[phase, me],
+                parts.at[me],
+                parts.at[me],
                 {"dep": dep if dp == 0 else other_chip, "tp": h if dh == 0 else 1 - h},
             )
             for dp, dh in ((0, 1), (1, 0), (1, 1))
         ]
 
-    def total_of(parts, phase):
-        return parts[phase, 0] + parts[phase, 1] + parts[phase, 2] + parts[phase, 3]
-
-    def inv_rms(phase):
-        return lax.rsqrt(total_of(square_parts, phase)[0:1, :] / D + EPS)
-
-    def start_squares(phase, squares):
-        square_parts[phase, p * 2 + h] = jnp.broadcast_to(squares, (8, ROWS))
-        return to_unit(square_parts, phase)
-
-    def start_gates(phase, hidden):
-        scaled = hidden * tgain_ref[my_columns].reshape(1, QUARTER)
-        logits = jnp.dot(scaled.astype(BF16), router_ref[p], preferred_element_type=F32).T
+    def total_of(parts):
+        return parts[0] + parts[1] + parts[2] + parts[3]
+
+    def chosen_logits(scaled, weight, ids):
+        logits = jnp.dot(scaled.astype(BF16), weight, preferred_element_type=F32).T
         expert = lax.broadcasted_iota(jnp.int32, (128, ROWS), 0)
-        ids = held_ids[0, phase * TOPK : (phase + 1) * TOPK]
-        me = p * 2 + h
-        for k in range(TOPK):
-            gate_parts[phase, me, k : k + 1, :] = jnp.sum(
-                jnp.where(ids[k : k + 1, :] == expert, logits, 0.0), 0, keepdims=True
-            )
-        return to_unit(gate_parts, phase)
-
-    def normalise(phase, hidden):
-        inverse = jnp.broadcast_to(inv_rms(phase), (ROWS, ROWS)).T[:, 0:1]
-        held[phase, 0] = (hidden * tgain_ref[my_columns].reshape(1, QUARTER) * inverse).astype(BF16)
-
-    def gate(phase):
-        chosen = total_of(gate_parts, phase) * inv_rms(phase)
+        return jnp.concatenate(
+            [
+                jnp.sum(jnp.where(ids[k : k + 1, :] == expert, logits, 0.0), 0, keepdims=True)
+                for k in range(TOPK)
+            ],
+            0,
+        )
+
+    def gate(chosen):
         raised = jnp.exp(chosen - jnp.max(chosen, 0, keepdims=True))
         return raised / jnp.sum(raised, 0, keepdims=True)
 
@@ -337,17 +340,8 @@
 
         lax.fori_loop(1, PLANE, send, 0)
 
-    def text_hidden():
-        return jnp.where(
-            flag((ROWS, QUARTER)),
-            text_peer[...].astype(F32),
-            text_ref[:, my_columns].astype(F32),
-        )
-
     def text_spread(*slots):
         for slot in slots:
-            if slot:
-                id_copies[NZ - 1 - slot].wait_recv()
             spread(TEXT, slot)
 
     def attend(lanes):
@@ -408,13 +402,19 @@
         part_copies.append(remote(part_send.at[block], part_recv.at[block], {"tp": 1 - h}))
     arrived(hop_b)
     hop_b = z_hop_b(2)
+    x_send_b(1, -1)
     arrived(across_x)
     hop_a = z_hop_a(1)
+    text_copy.wait_recv()
+    held[TEXT, 0] = jnp.where(
+        flag((ROWS, QUARTER)), text_peer[...].astype(F32), text_normed[:, my_columns].astype(F32)
+    ).astype(BF16)
+    ring = ring_hop(TEXT, 1)
+    text_spread(0)
     context = attend(my_rows)
-    text_copy.wait_recv()
-    hidden = text_hidden()
-    squares = jnp.broadcast_to(jnp.sum(hidden * hidden, 1, keepdims=True), (ROWS, ROWS))
-    text_squares = start_squares(TEXT, squares.T[0:1, :])
+    arrived(hop_b)
+    hop_b = z_hop_b(3)
+    x_send_b(2, -2)
     arrived(part_copies)
     for lo in range(0, V, 384):
         block = pl.ds(lo, 384)
@@ -427,14 +427,17 @@
     give = pl.ds(pl.multiple_of((1 - p) * 128, 128), 128)
     merged_copy = remote(merged.at[:, give], merged_peer, {"dep": other_chip})
 
-    arrived(text_squares)
-    normalise(TEXT, text_hidden())
-    ring = ring_hop(TEXT, 1)
-    text_spread(0)
     arrived(hop_b)
-    hop_b = z_hop_b(3)
+    hop_b = z_hop_b(4)
+    x_send_b(3, -3)
     arrived(hop_a)
     hop_a = z_hop_a(2)
+    arrived(ring)
+    ring = ring_hop(TEXT, 2)
+    arrived(id_copies)
+    text_spread(1, 7)
+    arrived(hop_b)
+    x_send_b(4)
     merged_copy.wait_recv()
     merged_mine[...] = jnp.where(
         flag((V, 128)), merged[:, keep].astype(F32), merged_peer[...].astype(F32)
@@ -448,13 +451,6 @@
         if step > 0:
             remote(own_half, place, {"dep": along_y(step)}, acts_recv)
         remote(theirs, place, {"dep": along_y(step), "tp": 1 - h}, acts_recv)
-    arrived(hop_b)
-    hop_b = z_hop_b(4)
-    arrived(ring)
-    ring = ring_hop(TEXT, 2)
-    text_spread(1, 7)
-    arrived(hop_b)
-    hop_b = x_hop_b(1)
     arrived(hop_a)
     hop_a = z_hop_a(3)
     arrived(ring)
@@ -462,15 +458,12 @@
     text_spread(2, 6)
     arrived(hop_a)
     hop_a = z_hop_a(4)
-    arrived(hop_b)
-    hop_b = x_hop_b(2)
     arrived(ring)
     ring = ring_hop(TEXT, 4)
-    text_spread(3, 5)
-    arrived(ring)
-    text_spread(4)
     loads[4].wait()
-    text_gates = start_gates(TEXT, text_hidden())
+    scaled = text_ref[...].astype(F32) * tgain_ref[...].reshape(1, 2 * QUARTER)
+    text_chosen[h] = chosen_logits(scaled, router_ref[...].reshape(2 * QUARTER, 128), ids_ref[...])
+    text_gates = remote(text_chosen.at[h], text_chosen.at[h], {"tp": 1 - h})
     for slot in range(NZ):
         plane_counts[pl.ds(lax.rem(z + slot, NZ), 1), :] = held_ids[slot, 2 * TOPK : 2 * TOPK + 1]
     all_counts[xy] = plane_counts[...]
@@ -488,8 +481,9 @@
 
     lax.fori_loop(1, PLANE, send_counts, 0)
     arrived(hop_a)
-    arrived(hop_b)
+    arrived(shared)
     pltpu.make_async_copy(acts, acts, acts_recv).wait()
+    text_spread(3)
 
     def columns_of(zs):
         total = None
@@ -517,25 +511,37 @@
     for step in range(1, NY):
         to_y = lax.rem(y + step, NY)
         remote(vis_block(to_y), vis_all.at[:, y], {"dep": along_y(step)}, vis_all_recv)
+    text_spread(5)
     pltpu.make_async_copy(vis_all, vis_all, vis_all_recv).wait()
 
     hidden = vis_all[...].reshape(QUARTER, ROWS).astype(F32)
-    image_squares = start_squares(IMAGE, jnp.sum(hidden * hidden, 0, keepdims=True))
-    image_rows[...] = hidden.T
+    me = p * 2 + h
+    square_parts[me] = jnp.broadcast_to(jnp.sum(hidden * hidden, 0, keepdims=True), (8, ROWS))
+    image_squares = to_unit(square_parts)
+    arrived(ring)
+    text_spread(4)
+    image_rows[...] = hidden.T * tgain_ref[my_columns].reshape(1, QUARTER)
     arrived(image_squares)
-    normalise(IMAGE, image_rows[...])
+    image_inverse = lax.rsqrt(total_of(square_parts)[0:1, :] / D + EPS)
+    inverse = jnp.broadcast_to(image_inverse, (ROWS, ROWS)).T[:, 0:1]
+    held[IMAGE, 0] = (image_rows[...] * inverse).astype(BF16)
     ring = ring_hop(IMAGE, 1)
     spread(IMAGE, 0)
-    image_gates = start_gates(IMAGE, image_rows[...])
+    gate_parts[me] = chosen_logits(image_rows[...], router_ref[p], held_ids[0, TOPK : 2 * TOPK])
+    image_gates = to_unit(gate_parts)
     for step in range(1, 5):
         arrived(ring)
         if step < 4:
             ring = ring_hop(IMAGE, step + 1)
         for slot in (step, NZ - step) if step < 4 else (4,):
             spread(IMAGE, slot)
-    arrived(text_gates)
+    text_gates.wait_recv()
     arrived(image_gates)
-    gate_ref[...] = jnp.where(flag((TOPK, ROWS)), gate(IMAGE), gate(TEXT))
+    gate_ref[...] = jnp.where(
+        flag((TOPK, ROWS)),
+        gate(total_of(gate_parts) * image_inverse),
+        gate((text_chosen[0] + text_chosen[1]) * text_inverse),
+    )
 
     for copy in started:
         copy.wait_send()
@@ -559,7 +565,7 @@
     loaded = (patches, text, proj, pout, merger, router)
     rows = NZ * PLANE // 2 * SLOTS
     buffer = pltpu.VMEM((rows, 2 * QUARTER), BF16)
-    copies = 96
+    copies = 112
     return pl.pallas_call(
         fused_kernel,
         out_shape=(
@@ -600,14 +606,17 @@
             pltpu.VMEM((8, NY, OWN_COLUMNS, ROWS), BF16),
             pltpu.VMEM((ROWS, QUARTER), F32),
             pltpu.VMEM((ROWS, QUARTER), BF16),
+            pltpu.VMEM((ROWS, 2 * QUARTER), BF16),
+            pltpu.VMEM((2, 8, ROWS), F32),
+            pltpu.VMEM((2, TOPK, ROWS), F32),
             pltpu.VMEM((TOPK, ROWS), jnp.int32),
             pltpu.VMEM((NZ, 2 * TOPK + 8, ROWS), jnp.int32),
             pltpu.VMEM((NZ, ROWS), jnp.int32),
             pltpu.VMEM((PLANE, NZ, ROWS), jnp.int32),
             pltpu.VMEM((2, NZ, ROWS, QUARTER), BF16),
             pltpu.VMEM((2, NZ, PLANE * SLOTS, QUARTER), BF16),
-            pltpu.VMEM((2, 4, 8, ROWS), F32),
-            pltpu.VMEM((2, 4, TOPK, ROWS), F32),
+            pltpu.VMEM((4, 8, ROWS), F32),
+            pltpu.VMEM((4, TOPK, ROWS), F32),
             pltpu.SemaphoreType.DMA((6,)),
             pltpu.SemaphoreType.DMA((copies,)),
             pltpu.SemaphoreType.DMA((copies,)),

time: 159 us -> 151 us (0.950)
  Pallas kernels: 157 us -> 149 us
    pallas_call x1, Pallas kernels: 153 us -> 145 us  [fused(): pl.pallas_call(fused_kernel, out_shape=(buffer, buffer, pltpu.VMEM((TOPK,...]
where the time goes in v5:
time: 151 us
  Pallas kernels  149 us (99%)
    pallas_call x1, Pallas kernels, fused(): pl.pallas_call(fused_kernel, out_shape=(buffer, buffer, pltpu.VMEM((TOPK,...  145 us
    pallas_call x1, Pallas kernels, interleave(): pl.pallas_call(interleave_kernel, out_shape=(jax.ShapeDtypeStruct((2 * te...  4.42 us

profile of v5, /device:TPU:1, one launch (start us, length us, event | category | flops | bytes accessed | tf_op | source)
XLA Modules:
  0.0 150.9 jit_solution(7443685263343915942)
XLA Ops:
  1.3 145.0 %shard_map.140 = (bf16[1024,2048]{1,0:T(8,128)(2,1)S(1)}, bf16[1024,2048]{1,0:T(8,128)(2,1)S(1)}, f32[8,128]{1,0:T(8,128)S(1)}, s32[8,128]{1,0:T(8,128)S(1)}) custom-call(s32[1]{0:T(128)S(6)} %copy.15.image_ref, bf16[576,512]{1,0:T(8,128)(2,1)} %bitcast.8, bf16[128,2048]{1,0:T(8,128)(2,1)} %text_hbm.1, s32[8,128]{1,0:T(8,128)} %bitcast.11, ...), custom_call_target="tpu_custom_call" | custom-call | tf_op jit(solution)/shard_map/pallas_call | solution.py:569
  146.3 4.4 %shard_map.141 = (bf16[2048,2048]{1,0:T(8,128)(2,1)}, f32[8,128]{1,0:T(8,128)}) custom-call(s32[8,128]{1,0:T(8,128)S(1)} %get-tuple-element.8.counts_ref, bf16[1024,2048]{1,0:T(8,128)(2,1)S(1)} %get-tuple-element.9.text_ref, bf16[1024,2048]{1,0:T(8,128)(2,1)S(1)} %get-tuple-element.10.image_ref, f32[8,128]{1,0:T(8,128)S(1)} %get-tuple-element.11.gate_ref), custom_call_target="tpu_custom_call" | custom-call | tf_op jit(solution)/shard_map/pallas_call | solution.py:658

commit v6 on v5

--- a/solution.py
+++ b/solution.py
@@ -393,6 +393,11 @@
 
     my_rows = pl.ds(pl.multiple_of(h * 256, 256), 256)
     their_rows = pl.ds(pl.multiple_of((1 - h) * 256, 256), 256)
+    arrived(hop_b)
+    hop_b = z_hop_b(2)
+    x_send_b(1, -1)
+    arrived(across_x)
+    hop_a = z_hop_a(1)
     context = attend(their_rows)
     loads[5].wait()
     part_copies = []
@@ -400,11 +405,6 @@
         part_send[lo : lo + 384, :] = out_product(context, lo)
         block = pl.ds(lo, 384)
         part_copies.append(remote(part_send.at[block], part_recv.at[block], {"tp": 1 - h}))
-    arrived(hop_b)
-    hop_b = z_hop_b(2)
-    x_send_b(1, -1)
-    arrived(across_x)
-    hop_a = z_hop_a(1)
     text_copy.wait_recv()
     held[TEXT, 0] = jnp.where(
         flag((ROWS, QUARTER)), text_peer[...].astype(F32), text_normed[:, my_columns].astype(F32)
@@ -433,7 +433,6 @@
     arrived(hop_a)
     hop_a = z_hop_a(2)
     arrived(ring)
-    ring = ring_hop(TEXT, 2)
     arrived(id_copies)
     text_spread(1, 7)
     arrived(hop_b)
@@ -453,13 +452,12 @@
         remote(theirs, place, {"dep": along_y(step), "tp": 1 - h}, acts_recv)
     arrived(hop_a)
     hop_a = z_hop_a(3)
-    arrived(ring)
-    ring = ring_hop(TEXT, 3)
-    text_spread(2, 6)
+    ring = ring_hop(TEXT, 2)
     arrived(hop_a)
     hop_a = z_hop_a(4)
     arrived(ring)
-    ring = ring_hop(TEXT, 4)
+    ring = ring_hop(TEXT, 3)
+    text_spread(2)
     loads[4].wait()
     scaled = text_ref[...].astype(F32) * tgain_ref[...].reshape(1, 2 * QUARTER)
     text_chosen[h] = chosen_logits(scaled, router_ref[...].reshape(2 * QUARTER, 128), ids_ref[...])
@@ -483,7 +481,7 @@
     arrived(hop_a)
     arrived(shared)
     pltpu.make_async_copy(acts, acts, acts_recv).wait()
-    text_spread(3)
+    text_spread(6)
 
     def columns_of(zs):
         total = None
@@ -497,10 +495,26 @@
     for c in range(2):
         vis_send[c] = columns_of((1 - h) * 4 + 2 * c)
         vis_copies.append(remote(vis_send.at[c], vis_recv.at[c], {"tp": 1 - h}))
+    squares = jnp.zeros((1, 2 * ROWS), F32)
     for c in range(2):
         product = columns_of(h * 4 + 2 * c)
         vis_copies[c].wait_recv()
-        vis[pl.ds(8 * c, 8)] = (product + vis_recv[c]).astype(BF16).reshape(8, OWN_COLUMNS, 256)
+        rounded = (product + vis_recv[c]).astype(BF16)
+        vis[pl.ds(8 * c, 8)] = rounded.reshape(8, OWN_COLUMNS, 256)
+        rounded = rounded.astype(F32)
+        squares = squares + jnp.sum(rounded * rounded, 0, keepdims=True)
+    core = 2 * y + h
+    square_parts[core] = jnp.broadcast_to(squares, (8, 2 * ROWS))
+    image_squares = [
+        remote(
+            square_parts.at[core],
+            square_parts.at[core],
+            {"dep": along_y(dy), "tp": h if dh == 0 else 1 - h},
+        )
+        for dy in range(NY)
+        for dh in range(2)
+        if dy + dh > 0
+    ]
 
     def vis_block(to_y):
         return vis.at[
@@ -511,22 +525,24 @@
     for step in range(1, NY):
         to_y = lax.rem(y + step, NY)
         remote(vis_block(to_y), vis_all.at[:, y], {"dep": along_y(step)}, vis_all_recv)
-    text_spread(5)
+    arrived(ring)
+    ring = ring_hop(TEXT, 4)
+    text_spread(3, 5)
     pltpu.make_async_copy(vis_all, vis_all, vis_all_recv).wait()
 
     hidden = vis_all[...].reshape(QUARTER, ROWS).astype(F32)
     me = p * 2 + h
-    square_parts[me] = jnp.broadcast_to(jnp.sum(hidden * hidden, 0, keepdims=True), (8, ROWS))
-    image_squares = to_unit(square_parts)
-    arrived(ring)
-    text_spread(4)
     image_rows[...] = hidden.T * tgain_ref[my_columns].reshape(1, QUARTER)
     arrived(image_squares)
-    image_inverse = lax.rsqrt(total_of(square_parts)[0:1, :] / D + EPS)
+    squares = sum(square_parts[core, 0:1, lanes] for core in range(2 * NY))
+    image_inverse = lax.rsqrt(squares / D + EPS)
     inverse = jnp.broadcast_to(image_inverse, (ROWS, ROWS)).T[:, 0:1]
     held[IMAGE, 0] = (image_rows[...] * inverse).astype(BF16)
+    last_text = ring
     ring = ring_hop(IMAGE, 1)
     spread(IMAGE, 0)
+    arrived(last_text)
+    text_spread(4)
     gate_parts[me] = chosen_logits(image_rows[...], router_ref[p], held_ids[0, TOPK : 2 * TOPK])
     image_gates = to_unit(gate_parts)
     for step in range(1, 5):
@@ -565,7 +581,7 @@
     loaded = (patches, text, proj, pout, merger, router)
     rows = NZ * PLANE // 2 * SLOTS
     buffer = pltpu.VMEM((rows, 2 * QUARTER), BF16)
-    copies = 112
+    copies = 128
     return pl.pallas_call(
         fused_kernel,
         out_shape=(
@@ -615,7 +631,7 @@
             pltpu.VMEM((PLANE, NZ, ROWS), jnp.int32),
             pltpu.VMEM((2, NZ, ROWS, QUARTER), BF16),
             pltpu.VMEM((2, NZ, PLANE * SLOTS, QUARTER), BF16),
-            pltpu.VMEM((4, 8, ROWS), F32),
+            pltpu.VMEM((2 * NY, 8, 2 * ROWS), F32),
             pltpu.VMEM((4, TOPK, ROWS), F32),
             pltpu.SemaphoreType.DMA((6,)),
             pltpu.SemaphoreType.DMA((copies,)),

time: 151 us -> 149 us (0.987)
  Pallas kernels: 149 us -> 147 us
    pallas_call x1, Pallas kernels: 145 us -> 143 us  [fused(): pl.pallas_call(fused_kernel, out_shape=(buffer, buffer, pltpu.VMEM((TOPK,...]
where the time goes in v6:
time: 149 us
  Pallas kernels  147 us (99%)
    pallas_call x1, Pallas kernels, fused(): pl.pallas_call(fused_kernel, out_shape=(buffer, buffer, pltpu.VMEM((TOPK,...  143 us
    pallas_call x1, Pallas kernels, interleave(): pl.pallas_call(interleave_kernel, out_shape=(jax.ShapeDtypeStruct((2 * te...  4.42 us

profile of v6, /device:TPU:1, one launch (start us, length us, event | category | flops | bytes accessed | tf_op | source)
XLA Modules:
  0.0 148.6 jit_solution(8216631326854137527)
XLA Ops:
  1.3 142.7 %shard_map.140 = (bf16[1024,2048]{1,0:T(8,128)(2,1)S(1)}, bf16[1024,2048]{1,0:T(8,128)(2,1)S(1)}, f32[8,128]{1,0:T(8,128)S(1)}, s32[8,128]{1,0:T(8,128)S(1)}) custom-call(s32[1]{0:T(128)S(6)} %copy.15.image_ref, bf16[576,512]{1,0:T(8,128)(2,1)} %bitcast.8, bf16[128,2048]{1,0:T(8,128)(2,1)} %text_hbm.1, s32[8,128]{1,0:T(8,128)} %bitcast.11, ...), custom_call_target="tpu_custom_call" | custom-call | tf_op jit(solution)/shard_map/pallas_call | solution.py:585
  144.0 4.4 %shard_map.141 = (bf16[2048,2048]{1,0:T(8,128)(2,1)}, f32[8,128]{1,0:T(8,128)}) custom-call(s32[8,128]{1,0:T(8,128)S(1)} %get-tuple-element.8.counts_ref, bf16[1024,2048]{1,0:T(8,128)(2,1)S(1)} %get-tuple-element.9.text_ref, bf16[1024,2048]{1,0:T(8,128)(2,1)S(1)} %get-tuple-element.10.image_ref, f32[8,128]{1,0:T(8,128)S(1)} %get-tuple-element.11.gate_ref), custom_call_target="tpu_custom_call" | custom-call | tf_op jit(solution)/shard_map/pallas_call | solution.py:674

commit v7 on v6

--- a/solution.py
+++ b/solution.py
@@ -432,11 +432,11 @@
     x_send_b(3, -3)
     arrived(hop_a)
     hop_a = z_hop_a(2)
+    arrived(hop_b)
+    x_send_b(4)
     arrived(ring)
     arrived(id_copies)
     text_spread(1, 7)
-    arrived(hop_b)
-    x_send_b(4)
     merged_copy.wait_recv()
     merged_mine[...] = jnp.where(
         flag((V, 128)), merged[:, keep].astype(F32), merged_peer[...].astype(F32)

time: 149 us -> 153 us (1.027)
  Pallas kernels: 147 us -> 151 us
    pallas_call x1, Pallas kernels: 143 us -> 147 us  [fused(): pl.pallas_call(fused_kernel, out_shape=(buffer, buffer, pltpu.VMEM((TOPK,...]
where the time goes in v7:
time: 153 us; the launch traced here: 152 us
  Pallas kernels  151 us (99%)
    pallas_call x1, Pallas kernels, fused(): pl.pallas_call(fused_kernel, out_shape=(buffer, buffer, pltpu.VMEM((TOPK,...  147 us
    pallas_call x1, Pallas kernels, interleave(): pl.pallas_call(interleave_kernel, out_shape=(jax.ShapeDtypeStruct((2 * te...  4.42 us

profile of v7, /device:TPU:1, one launch (start us, length us, event | category | flops | bytes accessed | tf_op | source)
XLA Modules:
  0.0 152.4 jit_solution(9550767014598480491)
XLA Ops:
  1.3 146.5 %shard_map.140 = (bf16[1024,2048]{1,0:T(8,128)(2,1)S(1)}, bf16[1024,2048]{1,0:T(8,128)(2,1)S(1)}, f32[8,128]{1,0:T(8,128)S(1)}, s32[8,128]{1,0:T(8,128)S(1)}) custom-call(s32[1]{0:T(128)S(6)} %copy.15.image_ref, bf16[576,512]{1,0:T(8,128)(2,1)} %bitcast.8, bf16[128,2048]{1,0:T(8,128)(2,1)} %text_hbm.1, s32[8,128]{1,0:T(8,128)} %bitcast.11, ...), custom_call_target="tpu_custom_call" | custom-call | tf_op jit(solution)/shard_map/pallas_call | solution.py:585
  147.8 4.4 %shard_map.141 = (bf16[2048,2048]{1,0:T(8,128)(2,1)}, f32[8,128]{1,0:T(8,128)}) custom-call(s32[8,128]{1,0:T(8,128)S(1)} %get-tuple-element.8.counts_ref, bf16[1024,2048]{1,0:T(8,128)(2,1)S(1)} %get-tuple-element.9.text_ref, bf16[1024,2048]{1,0:T(8,128)(2,1)S(1)} %get-tuple-element.10.image_ref, f32[8,128]{1,0:T(8,128)S(1)} %get-tuple-element.11.gate_ref), custom_call_target="tpu_custom_call" | custom-call | tf_op jit(solution)/shard_map/pallas_call | solution.py:674
